TPU v7x, 128 devices: a whole 4x4x4 slice. The times are simulated.
128 devices in a mesh: tm: 32 (over x, z, core), band: 4 (over y).
Axes of the slice: x: 4, y: 4, z: 4, core: 2. Of those that a mesh axis runs over, the one named last changes fastest.
Arguments:
- section_in: bfloat16 [64, 32, 8, 512], P('tm', 'band'), may hold values from -6 to 6
- norm_gain: float32 [512], replicated, may hold values from 0.1 to 1.9
- conv_weight: bfloat16 [3, 3, 3, 512, 512], replicated, may hold values from -0.0546875 to 0.0546875
- conv_bias: float32 [512], replicated, may hold values from -2 to 2
- lengths: int32 [4], replicated, may hold values from 1 to 48, as said below
- embed_weight: bfloat16 [512, 3072], replicated, may hold values from -0.25 to 0.25
- embed_bias: float32 [3072], replicated, may hold values from -3 to 3
- mod_shift: float32 [3072], replicated, may hold values from -3 to 3
- mod_scale: float32 [3072], replicated, may hold values from -1.5 to 1.5
- qkv_weight: bfloat16 [3072, 3, 12, 128], P(None, None, 'band'), may hold values from -0.109375 to 0.109375
- q_gain: float32 [128], replicated, may hold values from 1.2 to 6, as said below
- k_gain: float32 [128], replicated, may hold values from 1.2 to 6, as said below
Outputs:
- section_out: bfloat16 [64, 32, 8, 512], P('tm', 'band')
- attended: bfloat16 [16384, 12, 128], P('tm', 'band')
Inputs may be any that keep to these rules, and one draw needn't show every extreme that they name: `lengths`: whole frames of each clip; they sum to 64 and the longest clip has exactly 48 frames. `q_gain`: positive gains. `k_gain`: positive gains.
All inputs are finite; a program needn't handle non-finite values.
Results may differ from a plain program's by a relative error of at most 0.023.
The roundings to bfloat16 on the way count: a program that leaves them out, or rounds other values in their place, can miss the bound.
Values may be sent and summed in bfloat16 or wider, within the bound.
No kernel may reach another device: no remote copies, remote signals or barrier semaphores. Data moves between devices by JAX's collectives and lax.ppermute only.
A program may use at most 192 MiB of HBM per device.

v0:
```python
import functools

import jax
import jax.numpy as jnp
from jax import lax
from jax.experimental import pallas as pl
from jax.experimental.pallas import tpu as pltpu
from jax.sharding import PartitionSpec as P

EPSILON = 1e-06
NONE = -1e30
NX, NZ, NC, NB = 4, 4, 2, 4
HD = 128
FACTOR = 1.4426950408889634 / HD**0.5
HEADS = 3
SHARD = 128
FRAME = 256
OWN = 512
KEYS = 4096
F32 = jnp.float32
BF16 = jnp.bfloat16
MIB = 1024 * 1024


def params(mib):
    return pltpu.CompilerParams(vmem_limit_bytes=mib * MIB)


def fetch(sources, targets, sems, base=0):
    copies = [
        pltpu.make_async_copy(source, target, sems.at[base + at])
        for at, (source, target) in enumerate(zip(sources, targets))
    ]
    for copy in copies:
        copy.start()
    return copies


SMEM = pl.BlockSpec(memory_space=pltpu.SMEM)
VMEM = pl.BlockSpec(memory_space=pltpu.VMEM)
HBM = pl.BlockSpec(memory_space=pltpu.HBM)
ANY = pl.BlockSpec(memory_space=pl.ANY)


def pinned(*arrays):
    return [pltpu.with_memory_space_constraint(array, pltpu.HBM) for array in arrays]


def in_vmem(*arrays):
    return [pltpu.with_memory_space_constraint(array, pltpu.VMEM) for array in arrays]


def clip_of_frame(info_ref, frame):
    first, last, end = 0, 0, 0
    for clip in range(4):
        start, end = end, end + info_ref[clip]
        inside = (frame >= start) & (frame < end)
        first = jnp.where(inside, start, first)
        last = jnp.where(inside, end, last)
    return first, last


def place_of(info_ref):
    place = info_ref[4]
    return place // (NZ * NC), place // NC % NZ, place % NC


def split_bf16(value, count):
    parts = []
    for _ in range(count):
        part = value.astype(BF16).astype(F32)
        parts.append(part)
        value = value - part
    return parts


def after(array, *others):
    def kernel(source, *refs):
        (copy,) = fetch([source], [refs[-2]], refs[-1])
        copy.wait()

    return pl.pallas_call(
        kernel,
        in_specs=[ANY] * (1 + len(others)),
        out_specs=ANY,
        out_shape=jax.ShapeDtypeStruct(array.shape, array.dtype),
        scratch_shapes=[pltpu.SemaphoreType.DMA((1,))],
        compiler_params=params(2),
    )(array, *others)


def tm_index(x, z, c):
    return (x * NZ + z) * NC + c


def shift_tm(block, dx=0, dz=0, swap=False):
    route = []
    for x in range(NX):
        for z in range(NZ):
            for c in range(NC):
                target = tm_index((x + dx) % NX, (z + dz) % NZ, 1 - c if swap else c)
                route.append((tm_index(x, z, c), target))
    return lax.ppermute(block, "tm", route)


def shift_band(block, db):
    return lax.ppermute(block, "band", [(i, (i + db) % NB) for i in range(NB)])


def halo(block, dt, db):
    count = lax.axis_size("tm")
    route = []
    for t in range(count):
        for b in range(NB):
            if t + dt < count and 0 <= b + db < NB:
                route.append((t * NB + b, (t + dt) * NB + b + db))
    return lax.ppermute(block, ("tm", "band"), route)


def fold_kernel(
    embed_ref, bias_ref, shift_ref, scale_ref, gain_ref, qkv_ref, wq_ref, wk_ref, wv_ref, rows_ref, cols_ref,
    left,
):
    width = left.shape[1]
    gain = 1.0 + scale_ref[...]
    for lo in range(0, 512, 64):
        weight = embed_ref[lo : lo + 64, :].astype(F32)
        centred = weight - jnp.mean(weight, axis=-1, keepdims=True)
        left[lo : lo + 64, :] = (centred * gain).astype(BF16)
    bias = bias_ref[...]
    bias = (bias - jnp.mean(bias, axis=-1, keepdims=True)) * gain
    extra = jnp.zeros((16, width), F32)
    place = lax.broadcasted_iota(jnp.int32, (16, width), 0)
    for at, part in enumerate(split_bf16(bias, 3) + split_bf16(shift_ref[...], 3)):
        extra = jnp.where(place == at, part, extra)
    left[512:528, :] = extra.astype(BF16)
    where = lax.broadcasted_iota(jnp.int32, (8, HD), 0)
    cols_ref[2, 0:HD, :] = jnp.transpose(jnp.broadcast_to(gain_ref[...], (HD, HD)))
    for pair in ((0, 1), (2, 3), (4, 5), (6, 7), (8,)):
        right = jnp.concatenate([qkv_ref[i] for i in pair], axis=1)
        both = jnp.dot(left[...], right, preferred_element_type=F32)
        for at, block in enumerate(pair):
            part = both[:, at * HD : (at + 1) * HD]
            head = slice(block % HEADS * HD, (block % HEADS + 1) * HD)
            offset = part[512:513] + part[513:514] + part[514:515]
            moved = part[515:516] + part[516:517] + part[517:518]
            rows_ref[:, block * HD : (block + 1) * HD] = jnp.where(
                where == 0, offset, jnp.where(where == 1, moved, 0.0)
            )
            if block // HEADS == 0:
                wq_ref[:, head] = part[0:512].astype(BF16)
            elif block // HEADS == 1:
                wk_ref[head, :] = jnp.transpose(part[0:512]).astype(BF16)
                cols_ref[0, head, :] = jnp.transpose(jnp.broadcast_to(offset, (HD, HD)))
                cols_ref[1, head, :] = jnp.transpose(jnp.broadcast_to(moved, (HD, HD)))
            else:
                wv_ref[:, head] = part[0:512].astype(BF16)


def fold(embed_weight, embed_bias, mod_shift, mod_scale, k_gain, qkv):
    return pl.pallas_call(
        fold_kernel,
        in_specs=[VMEM] * 6,
        out_specs=[VMEM] * 5,
        out_shape=[
            jax.ShapeDtypeStruct((512, 384), BF16),
            jax.ShapeDtypeStruct((384, 512), BF16),
            jax.ShapeDtypeStruct((512, 384), BF16),
            jax.ShapeDtypeStruct((8, 1152), F32),
            jax.ShapeDtypeStruct((3, 384, HD), F32),
        ],
        scratch_shapes=[pltpu.VMEM((528, 3072), BF16)],
        compiler_params=params(16),
        cost_estimate=pl.CostEstimate(
            flops=2 * 528 * 3072 * 1152, bytes_accessed=12000000, transcendentals=0
        ),
    )(
        *in_vmem(embed_weight),
        embed_bias[None],
        mod_shift[None],
        mod_scale[None],
        k_gain[None],
        *in_vmem(qkv),
    )


def activate(cells, gain, act, slot, place):
    mean_square = jnp.mean(cells * cells, axis=-1, keepdims=True)
    scaled = cells * lax.rsqrt(mean_square + EPSILON) * gain
    active = (scaled * jax.nn.sigmoid(scaled)).astype(BF16).astype(F32)
    act[0, slot] = jnp.where(place == 0, 0.0, pltpu.roll(active, 1, 0))
    act[1, slot] = active
    act[2, slot] = jnp.where(place == 7, 0.0, pltpu.roll(active, 79, 0))


def newest_kernel(
    cur_ref, gain_hbm, weight_hbm, embed_hbm, qkv_hbm, part_ref, embed_out, qkv_out,
    act, gain_ref, weight_ref, sems,
):
    (gain_copy,) = fetch([gain_hbm], [gain_ref], sems)
    weight_copies = fetch(
        [weight_hbm.at[2, r] for r in range(3)], [weight_ref.at[r] for r in range(3)], sems, 1
    )
    copies = fetch((embed_hbm, qkv_hbm), (embed_out, qkv_out), sems, 4)
    place = lax.broadcasted_iota(jnp.int32, (80, 512), 0) % 8
    gain_copy.wait()
    for slot in range(2):
        activate(cur_ref[slot].astype(F32).reshape(80, 512), gain_ref[...], act, slot, place)
    total = jnp.zeros((SHARD, 512), F32)
    for tap_row in range(3):
        weight_copies[tap_row].wait()
        for tap_col in range(3):
            piece = jnp.concatenate(
                [act[tap_col, i, tap_row * 8 : tap_row * 8 + 64, :] for i in range(2)], axis=0
            ).astype(BF16)
            total = total + jnp.dot(
                piece, weight_ref[tap_row, tap_col], preferred_element_type=F32
            )
    part_ref[...] = total
    for copy in copies:
        copy.wait()


def conv_newest(cur, norm_gain, conv_weight, embed_weight, qkv):
    return pl.pallas_call(
        newest_kernel,
        in_specs=[VMEM] + [HBM] * 4,
        out_specs=[VMEM] + [ANY] * 2,
        out_shape=[
            jax.ShapeDtypeStruct((SHARD, 512), F32),
            jax.ShapeDtypeStruct(embed_weight.shape, BF16),
            jax.ShapeDtypeStruct(qkv.shape, BF16),
        ],
        scratch_shapes=[
            pltpu.VMEM((3, 2, 80, 512), F32),
            pltpu.VMEM((1, 512), F32),
            pltpu.VMEM((3, 3, 512, 512), BF16),
            pltpu.SemaphoreType.DMA((6,)),
        ],
        compiler_params=params(16),
        cost_estimate=pl.CostEstimate(
            flops=2 * 128 * 4608 * 512, bytes_accessed=15000000, transcendentals=0
        ),
    )(*in_vmem(cur), *pinned(norm_gain[None], conv_weight, embed_weight, qkv))


def conv_kernel(
    info_ref, cur_ref, prev_ref, part_ref, embed_ref, gain_hbm, bias_hbm, embed_bias_hbm, weight_hbm,
    out_ref, send_ref,
    act, gain_ref, bias_ref, embed_bias_ref, weight_ref, sems,
):
    copies = fetch(
        (gain_hbm, bias_hbm, embed_bias_hbm), (gain_ref, bias_ref, embed_bias_ref), sems
    )
    taps = [(t, r) for t in range(2) for r in range(3)]
    weight_copies = fetch(
        [weight_hbm.at[tap] for tap in taps], [weight_ref.at[tap] for tap in taps], sems, 3
    )
    first_frame = info_ref[4] * 2
    slots = []
    for i in range(2):
        clip_first, _ = clip_of_frame(info_ref, first_frame + i)
        slots.append(
            [jnp.maximum(first_frame + i - 2 + t, clip_first) - first_frame + 2 for t in range(2)]
        )
    place = lax.broadcasted_iota(jnp.int32, (80, 512), 0) % 8
    for copy in copies:
        copy.wait()
    for slot in range(4):
        cells = (prev_ref if slot < 2 else cur_ref)[slot % 2].astype(F32).reshape(80, 512)
        activate(cells, gain_ref[...], act, slot, place)
    inputs = jnp.concatenate(
        [cur_ref[i, 1:9].astype(F32).reshape(64, 512) for i in range(2)], axis=0
    )
    total = inputs + bias_ref[...] + part_ref[...]
    for at, (tap_time, tap_row) in enumerate(taps):
        weight_copies[at].wait()
        for tap_col in range(3):
            piece = jnp.concatenate(
                [
                    act[tap_col, slots[i][tap_time], tap_row * 8 : tap_row * 8 + 64, :]
                    for i in range(2)
                ],
                axis=0,
            ).astype(BF16)
            total = total + jnp.dot(
                piece, weight_ref[tap_time, tap_row, tap_col], preferred_element_type=F32
            )
    section = total.astype(BF16)
    out_ref[...] = section.reshape(out_ref.shape)
    send_ref[0:SHARD, :] = section
    embedded = jnp.dot(section, embed_ref[...], preferred_element_type=F32) + embed_bias_ref[...]
    center = embedded - jnp.mean(embedded, axis=-1, keepdims=True)
    spread = jnp.mean(center * center, axis=-1, keepdims=True)
    scale = lax.rsqrt(spread + EPSILON)
    across = jnp.transpose(jnp.broadcast_to(scale, (SHARD, SHARD)))[0:16]
    high, low = split_bf16(across, 2)
    tail = jnp.concatenate([high, low, jnp.zeros((16, 256), F32)], axis=1)
    place = lax.broadcasted_iota(jnp.int32, (16, 512), 0)
    send_ref[SHARD : SHARD + 16, :] = jnp.where(place == 0, tail, 0.0).astype(BF16)


def conv(info, cur, prev, part, norm_gain, conv_bias, embed_near, embed_bias, conv_weight):
    return pl.pallas_call(
        conv_kernel,
        in_specs=[SMEM] + [VMEM] * 4 + [HBM] * 4,
        out_specs=[VMEM] * 2,
        out_shape=[
            jax.ShapeDtypeStruct((2, 8, 8, 512), BF16),
            jax.ShapeDtypeStruct((SHARD + 16, 512), BF16),
        ],
        scratch_shapes=[
            pltpu.VMEM((3, 4, 80, 512), F32),
            pltpu.VMEM((1, 512), F32),
            pltpu.VMEM((1, 512), F32),
            pltpu.VMEM((1, 3072), F32),
            pltpu.VMEM((2, 3, 3, 512, 512), BF16),
            pltpu.SemaphoreType.DMA((9,)),
        ],
        compiler_params=params(24),
        cost_estimate=pl.CostEstimate(
            flops=2 * 128 * 13824 * 512, bytes_accessed=12000000, transcendentals=0
        ),
    )(
        info,
        *in_vmem(cur, prev, part, embed_near),
        *pinned(norm_gain[None], conv_bias[None], embed_bias[None], conv_weight),
    )


def normed(values, gain):
    mean_square = jnp.mean(values * values, axis=-1, keepdims=True)
    return (values * lax.rsqrt(mean_square + EPSILON) * gain).astype(BF16)


def query_kernel(
    band_ref, s0, s1, s3, s2, weight_ref, rows_ref, gain_ref, q_ref, xr_ref
):
    band = band_ref[5]
    across = []
    sources = []
    for back, ref in ((0, s0), (1, s1), (3, s3), (2, s2)):
        source = lax.rem(band + (NB - back), NB)
        sources.append(source)
        cells = ref[0:SHARD, :]
        extra = ref[SHARD : SHARD + 16, :].astype(F32)[0:1]
        across.append(extra)
        scale = jnp.transpose(jnp.broadcast_to(extra[:, 0:HD] + extra[:, HD : 2 * HD], (HD, HD)))
        projected = (
            jnp.dot(cells, weight_ref[...], preferred_element_type=F32) + rows_ref[0:1, 0:384]
        )
        for head in range(HEADS):
            lanes = slice(head * HD, (head + 1) * HD)
            values = normed(projected[:, lanes] * scale + rows_ref[1:2, lanes], gain_ref[...])
            for i in range(2):
                rows = pl.ds(pl.multiple_of(i * FRAME + source * 64, 64), 64)
                q_ref[head, rows, :] = values[i * 64 : (i + 1) * 64]
        for i in range(2):
            rows = pl.ds(pl.multiple_of(i * FRAME + source * 64, 64), 64)
            xr_ref[rows, :] = cells[i * 64 : (i + 1) * 64]
    lines = []
    for term in range(2):
        pieces = []
        for i in range(2):
            for b in range(NB):
                lanes = slice(term * HD + i * 64, term * HD + (i + 1) * 64)
                piece = across[0][:, lanes]
                for source, extra in zip(sources[1:], across[1:]):
                    piece = jnp.where(source == b, extra[:, lanes], piece)
                pieces.append(piece)
        lines.append(jnp.concatenate(pieces, axis=1))
    place = lax.broadcasted_iota(jnp.int32, (16, 512), 0)
    tail = jnp.where(place == 0, lines[0], jnp.where(place == 1, lines[1], 0.0))
    xr_ref[OWN : OWN + 16, :] = tail.astype(BF16)


def queries_of(band, shards, weight, rows, gain):
    return pl.pallas_call(
        query_kernel,
        in_specs=[SMEM] + [VMEM] * 7,
        out_specs=[VMEM, VMEM],
        out_shape=[
            jax.ShapeDtypeStruct((HEADS, OWN, HD), BF16),
            jax.ShapeDtypeStruct((OWN + 16, 512), BF16),
        ],
        compiler_params=params(8),
        cost_estimate=pl.CostEstimate(
            flops=2 * 512 * 512 * 384, bytes_accessed=2000000, transcendentals=0
        ),
    )(band, *in_vmem(*shards, weight, rows), gain[None] * FACTOR)


def store_rows(o_ref, base, results):
    lane = lax.broadcasted_iota(jnp.int32, (FRAME, HD), 1)
    marks = jnp.zeros((FRAME, HD), F32)
    for head, (mixed, peak, weight_sum) in enumerate(results):
        some = weight_sum > 0.0
        safe = jnp.where(some, weight_sum, 1.0)
        o_ref[pl.ds(pl.multiple_of(head * OWN + base, FRAME), FRAME), :] = (mixed / safe).astype(
            BF16
        )
        level = jnp.where(some, peak + jnp.log2(safe), NONE)
        marks = jnp.where(lane == head, level, marks)
    for half in range(2):
        turned = jnp.transpose(marks[half * HD : (half + 1) * HD])[0:8]
        first, second, third = split_bf16(turned, 3)
        at = pl.multiple_of(HEADS * OWN + (base // HD + half) * 32, 32)
        tail = jnp.concatenate([first, second, third, jnp.zeros((8, HD), F32)], axis=0)
        o_ref[pl.ds(at, 32), :] = tail.astype(BF16)


LONG = 12
SHORT = 4


def attend_group(info_ref, group, q_ref, o_ref, key_t, value):
    x_here, z_here, core = place_of(info_ref)
    group_frame = x_here * 16 + lax.rem(z_here + NZ - group, NZ) * 4 + core * 2

    def bounds(i):
        ends = []
        for edge in clip_of_frame(info_ref, group_frame + i):
            inside = [jnp.clip(edge - 16 * x - 4 * z_here, 0, 4) for x in range(NX)]
            ends.append(inside[0] + inside[1] + inside[2] + inside[3])
        return ends[0], ends[1] - ends[0]

    def rows_of(start, frames, base, shown=None):
        width = frames * FRAME
        start = pl.multiple_of(start * FRAME, FRAME)

        def scores_of(head):
            return jnp.dot(
                q_ref[head, pl.ds(base, FRAME), :],
                key_t[head, :, pl.ds(start, width)],
                preferred_element_type=F32,
            )

        scores = scores_of(0)
        results = []
        for head in range(HEADS):
            ahead = scores_of(head + 1) if head + 1 < HEADS else None
            if shown is not None:
                scores = jnp.where(shown, scores, NONE)
            top = jnp.max(scores, axis=-1, keepdims=True)
            weights = jnp.exp2(scores - top)
            if shown is not None:
                weights = jnp.where(shown, weights, 0.0)
            weight_sum = jnp.sum(weights, axis=-1, keepdims=True)
            mixed = jnp.dot(
                weights.astype(BF16),
                value[head, pl.ds(start, width), :],
                preferred_element_type=F32,
            )
            results.append((mixed, top, weight_sum))
            scores = ahead
        store_rows(o_ref, base, results)

    def one_frame(i, carry):
        first, count = bounds(i)
        base = pl.multiple_of(i * FRAME, FRAME)

        @pl.when(count == LONG)
        def _():
            rows_of(first, LONG, base)

        @pl.when(count != LONG)
        def _():
            start = jnp.minimum(first, KEYS // FRAME - SHORT)
            lane = lax.broadcasted_iota(jnp.int32, (FRAME, SHORT * FRAME), 1)
            low = (first - start) * FRAME
            rows_of(start, SHORT, base, (lane >= low) & (lane < low + count * FRAME))

        return carry

    lax.fori_loop(0, 2, one_frame, 0)


def project_block(ref, start, wk_ref, wv_ref, rows_ref, cols_ref, key_t, value):
    cells = ref[0:OWN, :]
    extra = ref[OWN : OWN + 16, :].astype(F32)
    scale = extra[0:1] + extra[1:2]
    keys = lax.dot_general(
        wk_ref[...], cells, (((1,), (1,)), ((), ())), preferred_element_type=F32
    )
    for head in range(HEADS):
        lanes = slice(head * HD, (head + 1) * HD)
        offset = jnp.concatenate([cols_ref[0, lanes, :]] * 4, axis=1)
        moved = jnp.concatenate([cols_ref[1, lanes, :]] * 4, axis=1)
        gain = jnp.concatenate([cols_ref[2, 0:HD, :]] * 4, axis=1)
        part = (keys[lanes] + offset) * scale + moved
        mean_square = jnp.mean(part * part, axis=0, keepdims=True)
        key_t[head, :, pl.ds(start, OWN)] = (
            part * lax.rsqrt(mean_square + EPSILON) * gain
        ).astype(BF16)
    down = jnp.concatenate(
        [
            jnp.transpose(jnp.broadcast_to(scale[:, j * HD : (j + 1) * HD], (HD, HD)))
            for j in range(4)
        ],
        axis=0,
    )
    values = jnp.dot(cells, wv_ref[...], preferred_element_type=F32) + rows_ref[0:1, 768:1152]
    for head in range(HEADS):
        lanes = slice(head * HD, (head + 1) * HD)
        value[head, pl.ds(start, OWN), :] = (
            values[:, lanes] * down + rows_ref[1:2, 768 + head * HD : 768 + (head + 1) * HD]
        ).astype(BF16)


def first_kernel(
    info_ref, q_hbm, a0, b0, a1, b1, a3, b3, a2, b2, wk_hbm, wv_hbm, rows_hbm, cols_hbm,
    o2, key_out, value_out, key_t, value, blocks, q2, wk_ref, wv_ref, rows_ref, cols_ref,
    sems,
):
    x_here, _, core = place_of(info_ref)
    weight_copies = fetch(
        (wk_hbm, wv_hbm, rows_hbm, cols_hbm), (wk_ref, wv_ref, rows_ref, cols_ref), sems
    )
    sources = (a0, b0, a1, b1, a3, b3, a2, b2)
    block_copies = fetch(sources, [blocks.at[i] for i in range(8)], sems, 4)
    (query_copy,) = fetch([q_hbm], [q2], sems, 12)
    for copy in weight_copies:
        copy.wait()
    for at in range(8):
        if at % 4 == 0:
            for copy in block_copies[at : at + 4]:
                copy.wait()
        source = lax.rem(x_here + (NX - (0, 1, 3, 2)[at // 2]), NX)
        core_at = core if at % 2 == 0 else 1 - core
        start = pl.multiple_of((source * 2 + core_at) * OWN, OWN)
        project_block(blocks.at[at], start, wk_ref, wv_ref, rows_ref, cols_ref, key_t, value)
    copies = fetch((key_t, value), (key_out, value_out), sems, 13)
    query_copy.wait()
    attend_group(info_ref, 2, q2, o2, key_t, value)
    for copy in copies:
        copy.wait()


PARTIAL = jax.ShapeDtypeStruct((HEADS * OWN + 128, HD), BF16)


def attend_first(info, query, near, far, wk, wv, rows, cols):
    return pl.pallas_call(
        first_kernel,
        in_specs=[SMEM] + [ANY] * 13,
        out_specs=[VMEM, ANY, ANY],
        out_shape=[
            PARTIAL,
            jax.ShapeDtypeStruct((HEADS, HD, KEYS), BF16),
            jax.ShapeDtypeStruct((HEADS, KEYS, HD), BF16),
        ],
        scratch_shapes=[
            pltpu.VMEM((HEADS, HD, KEYS), BF16),
            pltpu.VMEM((HEADS, KEYS, HD), BF16),
            pltpu.VMEM((8, OWN + 16, 512), BF16),
            pltpu.VMEM((HEADS, OWN, HD), BF16),
            pltpu.VMEM((384, 512), BF16),
            pltpu.VMEM((512, 384), BF16),
            pltpu.VMEM((8, 1152), F32),
            pltpu.VMEM((3, 384, HD), F32),
            pltpu.SemaphoreType.DMA((15,)),
        ],
        compiler_params=params(34),
        cost_estimate=pl.CostEstimate(
            flops=15000000000, bytes_accessed=10000000, transcendentals=0
        ),
    )(
        info,
        query,
        *[block for pair in zip(near, far) for block in pair],
        wk,
        wv,
        rows,
        cols,
    )


def next_kernel(groups, info_ref, key_t, value, *refs):
    count = len(groups)
    sources, refs = refs[:count], refs[-(count + 3) :]
    outs, queries, partial, sems = refs[:count], refs[count], refs[count + 1], refs[count + 2]
    for copy in fetch(sources, [queries.at[n] for n in range(count)], sems):
        copy.wait()

    def one_group(n, carry):
        group = groups[0] + n * 2
        attend_group(info_ref, group, queries.at[n], partial.at[n], key_t, value)
        return carry

    lax.fori_loop(0, count, one_group, 0)
    for copy in fetch([partial.at[n] for n in range(count)], outs, sems, count):
        copy.wait()


def attend_next(groups, info, queries, key_t, value, *needed):
    key_t, value = [
        pltpu.with_memory_space_constraint(array, pltpu.VMEM) for array in (key_t, value)
    ]
    return pl.pallas_call(
        functools.partial(next_kernel, groups),
        in_specs=[SMEM, VMEM, VMEM] + [ANY] * (len(groups) + len(needed)),
        out_specs=[ANY] * len(groups),
        out_shape=[PARTIAL] * len(groups),
        scratch_shapes=[
            pltpu.VMEM((len(groups), HEADS, OWN, HD), BF16),
            pltpu.VMEM((len(groups), *PARTIAL.shape), BF16),
            pltpu.SemaphoreType.DMA((2 * len(groups),)),
        ],
        compiler_params=params(28),
        cost_estimate=pl.CostEstimate(
            flops=8000000000 * len(groups), bytes_accessed=8000000, transcendentals=0
        ),
    )(info, key_t, value, *queries, *needed)


def merge_kernel(p0, p1, p2, p3, out_ref):
    parts = (p0, p1, p2, p3)
    for at in range(4):
        base = HEADS * OWN + at * 32
        levels = []
        for ref in parts:
            marks = ref[base : base + 32, :].astype(F32)
            levels.append(marks[0:8] + marks[8:16] + marks[16:24])
        top = functools.reduce(jnp.maximum, levels)
        shares = [jnp.exp2(level - top) for level in levels]
        weight_sum = functools.reduce(jnp.add, shares)
        stacked = jnp.concatenate([share / weight_sum for share in shares], axis=0)
        columns = jnp.transpose(
            jnp.concatenate([stacked, jnp.zeros((HD - 32, HD), F32)], axis=0)
        )
        for head in range(HEADS):
            rows = slice(head * OWN + at * HD, head * OWN + (at + 1) * HD)
            mixed = functools.reduce(
                jnp.add,
                [
                    ref[rows, :].astype(F32) * columns[:, i * 8 + head : i * 8 + head + 1]
                    for i, ref in enumerate(parts)
                ],
            )
            out_ref[head, at * HD : (at + 1) * HD, :] = mixed.astype(BF16)


def merge(parts):
    return pl.pallas_call(
        merge_kernel,
        in_specs=[VMEM] * 4,
        out_specs=VMEM,
        out_shape=jax.ShapeDtypeStruct((HEADS, OWN, HD), BF16),
        compiler_params=params(8),
    )(*in_vmem(*parts))


def per_device(
    section_in,
    norm_gain,
    conv_weight,
    conv_bias,
    lengths,
    embed_weight,
    embed_bias,
    mod_shift,
    mod_scale,
    qkv_weight,
    q_gain,
    k_gain,
):
    info = jnp.concatenate(
        [lengths, jnp.stack([lax.axis_index("tm"), lax.axis_index("band")])]
    ).astype(jnp.int32)
    above = halo(section_in[:, 7:8], 0, 1)
    below = halo(section_in[:, 0:1], 0, -1)
    cur = jnp.concatenate([above, section_in, below], axis=1)
    prev = halo(cur, 1, 0)
    qkv = jnp.transpose(qkv_weight, (1, 2, 0, 3)).reshape(9, 3072, HD)
    part, embed_near, qkv_near = conv_newest(cur, norm_gain, conv_weight, embed_weight, qkv)
    section_out, send = conv(
        info, cur, prev, part, norm_gain, conv_bias, embed_near, embed_bias, conv_weight
    )
    wq, wk, wv, rows, cols = fold(
        embed_near, embed_bias, mod_shift, mod_scale, k_gain, qkv_near
    )
    shards = (send, shift_band(send, 1), shift_band(send, 3), shift_band(send, 2))
    query, xr = queries_of(
        info, shards, wq, rows, q_gain
    )
    far_own = shift_tm(xr, swap=True)
    a1, a3 = shift_tm(xr, dx=1), shift_tm(xr, dx=3)
    q1, q3, q2 = shift_tm(query, dz=1), shift_tm(query, dz=3), shift_tm(query, dz=2)
    a2 = after(shift_tm(xr, dx=2), q1, q3, q2)
    near = (xr, a1, a3, a2)
    far = (far_own,) + tuple(shift_tm(part, swap=True) for part in near[1:])
    o2, key_t, value = attend_first(info, q2, near, far, wk, wv, rows, cols)
    p2 = shift_tm(o2, dz=2)
    o1, o3 = attend_next((1, 3), info, (q1, q3), key_t, value)
    p1, p3 = shift_tm(o1, dz=3), shift_tm(o3, dz=1)
    (o0,) = attend_next((0,), info, (query,), key_t, value, p2)
    parts = (o0, p1, p3, p2)
    attended = jnp.transpose(merge(parts), (1, 0, 2))
    return (section_out, attended)


def solution(mesh):
    return jax.shard_map(
        per_device,
        mesh=mesh,
        in_specs=(
            P("tm", "band", None, None),
            P(),
            P(),
            P(),
            P(),
            P(),
            P(),
            P(),
            P(),
            P(None, None, "band", None),
            P(),
            P(),
        ),
        out_specs=(P("tm", "band", None, None), P("tm", "band", None)),
        check_vma=False,
    )
```

profile of v0, /device:TPU:2, one launch (start us, length us, event | category | flops | bytes accessed | tf_op | source)
XLA Modules:
  0.0 116.0 jit_solution(7089949526453097960)
XLA Ops:
  1.4 1.3 %collective-permute-start.1 = (bf16[2,1,8,512]{3,2,1,0:T(8,128)(2,1)S(1)}, bf16[2,1,8,512]{3,2,1,0:T(8,128)(2,1)S(1)}, u32[]{:S(2)}, u32[]{:S(2)}) collective-permute-start(bf16[2,1,8,512]{3,2,1,0:T(8,128)(2,1)S(1)} %get-tuple-element.36), channel_id=1, source_target_pairs={{1,0},{2,1},{3,2},{5,4},{6,5},{7,6},{9,8},{10,9},{11,10},{13,12},{... | collective-permute-start | bytes 49160 | tf_op jit(solution)/shard_map/ppermute | solution.py:117
  2.7 4.5 %collective-permute-start = (bf16[2,1,8,512]{3,2,1,0:T(8,128)(2,1)S(1)}, bf16[2,1,8,512]{3,2,1,0:T(8,128)(2,1)S(1)}, u32[]{:S(2)}, u32[]{:S(2)}) collective-permute-start(bf16[2,1,8,512]{3,2,1,0:T(8,128)(2,1)S(1)} %get-tuple-element.37), channel_id=1, source_target_pairs={{0,1},{1,2},{2,3},{4,5},{5,6},{6,7},{8,9},{9,10},{10,11},{12,13},{... | collective-permute-start | bytes 49160 | tf_op jit(solution)/shard_map/ppermute | solution.py:117
  7.9 0.8 collective-permute-done
  8.6 0.9 constant_dynamic-update-slice_fusion.1
  9.6 1.9 %collective-permute-start.2 = (bf16[2,10,8,512]{3,2,1,0:T(8,128)(2,1)S(1)}, bf16[2,10,8,512]{3,2,1,0:T(8,128)(2,1)S(1)}, u32[]{:S(2)}, u32[]{:S(2)}) collective-permute-start(bf16[2,10,8,512]{3,2,1,0:T(8,128)(2,1)S(1)} %constant_dynamic-update-slice_fusion.cur_ref), channel_id=1, source_target_pairs={{0,4},{1,5},{2,6},{3,7},{4,8},{5,9},{6,10},{7,11},{8,12},{9,13},{1... | collective-permute-start | bytes 491528 | tf_op jit(solution)/shard_map/ppermute | solution.py:117
  12.2 5.4 %shard_map.131 = (f32[128,512]{1,0:T(8,128)S(1)}, bf16[512,3072]{1,0:T(8,128)(2,1)S(1)}, bf16[9,3072,128]{2,1,0:T(8,128)(2,1)S(1)}) custom-call(bf16[2,10,8,512]{3,2,1,0:T(8,128)(2,1)S(1)} %constant_dynamic-update-slice_fusion.cur_ref, f32[1,512]{1,0:T(1,128)} %bitcast.21, bf16[3,3,3,512,512]{4,3,2,1,0:T(8,128)(2,1)} %weight_hbm.3, ...), custom_call_target="tpu_custom_call" | custom-call | flops 603979776 | bytes 15000000 | tf_op jit(solution)/shard_map/pallas_call | solution.py:225
  18.3 5.8 %shard_map.132 = (bf16[2,8,8,512]{3,2,1,0:T(8,128)(2,1)}, bf16[144,512]{1,0:T(8,128)(2,1)S(1)}) custom-call(s32[6]{0:T(128)S(1)} %pad_add_fusion.info_ref.band_ref, bf16[2,10,8,512]{3,2,1,0:T(8,128)(2,1)S(1)} %constant_dynamic-update-slice_fusion.cur_ref, bf16[2,10,8,512]{3,2,1,0:T(8,128)(2,1)S(1)} %collective-permute-done.2.prev_ref, ...), custom_call_target="tpu_custom_call" | custom-call | flops 1811939328 | bytes 12000000 | tf_op jit(solution)/shard_map/pallas_call | solution.py:304
  24.2 4.0 %collective-permute-start.5 = (bf16[144,512]{1,0:T(8,128)(2,1)S(1)}, bf16[144,512]{1,0:T(8,128)(2,1)S(1)}, u32[]{:S(2)}, u32[]{:S(2)}) collective-permute-start(bf16[144,512]{1,0:T(8,128)(2,1)S(1)} %get-tuple-element.22.s0), channel_id=1, source_target_pairs={{0,2},{1,3},{2,0},{3,1},{4,6},{5,7},{6,4},{7,5},{8,10},{9,11},{10,... | collective-permute-start | bytes 442376 | tf_op jit(solution)/shard_map/ppermute | solution.py:107
  28.2 1.1 collective-permute-start.4
  29.2 1.0 collective-permute-start.3
  30.2 5.0 %shard_map.133 = (bf16[512,384]{1,0:T(8,128)(2,1)S(1)}, bf16[384,512]{1,0:T(8,128)(2,1)S(1)}, bf16[512,384]{1,0:T(8,128)(2,1)S(1)}, f32[8,1152]{1,0:T(8,128)S(1)}, f32[3,384,128]{2,1,0:T(8,128)S(1)}) custom-call(bf16[512,3072]{1,0:T(8,128)(2,1)S(1)} %get-tuple-element.20.embed_ref, f32[1,3072]{1,0:T(1,128)S(1)} %bitcast.15, f32[1,3072]{1,0:T(1,128)S(1)} %bitcast.16, ...), custom_call_target="tpu_custom_call" | custom-call | flops 3737124864 | bytes 12000000 | tf_op jit(solution)/shard_map/pallas_call | solution.py:161
  35.2 1.4 %collective-permute-done.4.s3 = bf16[144,512]{1,0:T(8,128)(2,1)S(1)} collective-permute-done((bf16[144,512]{1,0:T(8,128)(2,1)S(1)}, bf16[144,512]{1,0:T(8,128)(2,1)S(1)}, u32[]{:S(2)}, u32[]{:S(2)}) %collective-permute-start.4) | collective-permute-done | bytes 147488 | tf_op jit(solution)/shard_map/ppermute | solution.py:107
  37.0 1.1 shard_map.134
  38.1 2.8 %collective-permute-start.14 = (bf16[3,512,128]{2,1,0:T(8,128)(2,1)S(1)}, bf16[3,512,128]{2,1,0:T(8,128)(2,1)S(1)}, u32[]{:S(2)}, u32[]{:S(2)}) collective-permute-start(bf16[3,512,128]{2,1,0:T(8,128)(2,1)S(1)} %get-tuple-element.26.refs_0_), channel_id=1, source_target_pairs={{0,24},{4,28},{8,0},{12,4},{16,8},{20,12},{24,16},{28,20},{32,56},... | collective-permute-start | bytes 1179656 | tf_op jit(solution)/shard_map/ppermute | solution.py:103
  40.9 1.4 %collective-permute-start.12 = (bf16[528,512]{1,0:T(8,128)(2,1)S(1)}, bf16[528,512]{1,0:T(8,128)(2,1)S(1)}, u32[]{:S(2)}, u32[]{:S(2)}) collective-permute-start(bf16[528,512]{1,0:T(8,128)(2,1)S(1)} %get-tuple-element.27.a0), channel_id=1, source_target_pairs={{0,64},{4,68},{8,72},{12,76},{16,80},{20,84},{24,88},{28,92},{32,9... | collective-permute-start | bytes 1622024 | tf_op jit(solution)/shard_map/ppermute | solution.py:103
  42.3 1.8 %collective-permute-start.10 = (bf16[528,512]{1,0:T(8,128)(2,1)S(1)}, bf16[528,512]{1,0:T(8,128)(2,1)S(1)}, u32[]{:S(2)}, u32[]{:S(2)}) collective-permute-start(bf16[528,512]{1,0:T(8,128)(2,1)S(1)} %get-tuple-element.27.a0), channel_id=1, source_target_pairs={{0,96},{4,100},{8,104},{12,108},{16,112},{20,116},{24,120},{28,124... | collective-permute-start | bytes 1622024 | tf_op jit(solution)/shard_map/ppermute | solution.py:103
  44.4 5.0 %collective-permute-done.14.refs_1_ = bf16[3,512,128]{2,1,0:T(8,128)(2,1)S(1)} collective-permute-done((bf16[3,512,128]{2,1,0:T(8,128)(2,1)S(1)}, bf16[3,512,128]{2,1,0:T(8,128)(2,1)S(1)}, u32[]{:S(2)}, u32[]{:S(2)}) %collective-permute-start.14) | collective-permute-done | bytes 393248 | tf_op jit(solution)/shard_map/ppermute | solution.py:103
  49.3 3.2 %collective-permute-start.6 = (bf16[3,512,128]{2,1,0:T(8,128)(2,1)S(1)}, bf16[3,512,128]{2,1,0:T(8,128)(2,1)S(1)}, u32[]{:S(2)}, u32[]{:S(2)}) collective-permute-start(bf16[3,512,128]{2,1,0:T(8,128)(2,1)S(1)} %get-tuple-element.26.refs_0_), channel_id=1, source_target_pairs={{0,16},{4,20},{8,24},{12,28},{16,0},{20,4},{24,8},{28,12},{32,48},... | collective-permute-start | bytes 1179656 | tf_op jit(solution)/shard_map/ppermute | solution.py:103
  52.6 3.2 %collective-permute-done.13.refs_0_ = bf16[3,512,128]{2,1,0:T(8,128)(2,1)S(1)} collective-permute-done((bf16[3,512,128]{2,1,0:T(8,128)(2,1)S(1)}, bf16[3,512,128]{2,1,0:T(8,128)(2,1)S(1)}, u32[]{:S(2)}, u32[]{:S(2)}) %collective-permute-start.13) | collective-permute-done | bytes 393248 | tf_op jit(solution)/shard_map/ppermute | solution.py:103
  55.7 8.3 %collective-permute-done.6.refs_2_.q_hbm = bf16[3,512,128]{2,1,0:T(8,128)(2,1)S(1)} collective-permute-done((bf16[3,512,128]{2,1,0:T(8,128)(2,1)S(1)}, bf16[3,512,128]{2,1,0:T(8,128)(2,1)S(1)}, u32[]{:S(2)}, u32[]{:S(2)}) %collective-permute-start.6) | collective-permute-done | bytes 393248 | tf_op jit(solution)/shard_map/ppermute | solution.py:103
  64.1 1.9 %collective-permute-done.10.a3 = bf16[528,512]{1,0:T(8,128)(2,1)S(1)} collective-permute-done((bf16[528,512]{1,0:T(8,128)(2,1)S(1)}, bf16[528,512]{1,0:T(8,128)(2,1)S(1)}, u32[]{:S(2)}, u32[]{:S(2)}) %collective-permute-start.10) | collective-permute-done | bytes 540704 | tf_op jit(solution)/shard_map/ppermute | solution.py:103
  66.7 1.2 %collective-permute-done.11.b3 = bf16[528,512]{1,0:T(8,128)(2,1)S(1)} collective-permute-done((bf16[528,512]{1,0:T(8,128)(2,1)S(1)}, bf16[528,512]{1,0:T(8,128)(2,1)S(1)}, u32[]{:S(2)}, u32[]{:S(2)}) %collective-permute-start.11) | collective-permute-done | bytes 540704 | tf_op jit(solution)/shard_map/ppermute | solution.py:103
  68.0 0.8 collective-permute-done.9.b1
  68.7 13.7 %shard_map.136 = (bf16[1664,128]{1,0:T(8,128)(2,1)S(1)}, bf16[3,128,4096]{2,1,0:T(8,128)(2,1)S(1)}, bf16[3,4096,128]{2,1,0:T(8,128)(2,1)S(1)}) custom-call(s32[6]{0:T(128)S(1)} %pad_add_fusion.info_ref.band_ref, bf16[3,512,128]{2,1,0:T(8,128)(2,1)S(1)} %collective-permute-done.6.refs_2_.q_hbm, bf16[528,512]{1,0:T(8,128)(2,1)S(1)} %get-tuple-element.27.a0, ...), custom_call_target="tpu_custom_call" | custom-call | flops 15000000512 | bytes 10000000 | tf_op jit(solution)/shard_map/pallas_call | solution.py:543
  82.4 3.2 %collective-permute-start.16 = (bf16[1664,128]{1,0:T(8,128)(2,1)S(1)}, bf16[1664,128]{1,0:T(8,128)(2,1)S(1)}, u32[]{:S(2)}, u32[]{:S(2)}) collective-permute-start(bf16[1664,128]{1,0:T(8,128)(2,1)S(1)} %get-tuple-element.33), channel_id=1, source_target_pairs={{0,16},{4,20},{8,24},{12,28},{16,0},{20,4},{24,8},{28,12},{32,48},... | collective-permute-start | bytes 1277960 | tf_op jit(solution)/shard_map/ppermute | solution.py:103
  85.6 14.7 %shard_map.138 = (bf16[1664,128]{1,0:T(8,128)(2,1)S(1)}, bf16[1664,128]{1,0:T(8,128)(2,1)S(1)}) custom-call(s32[6]{0:T(128)S(1)} %pad_add_fusion.info_ref.band_ref, bf16[3,128,4096]{2,1,0:T(8,128)(2,1)S(1)} %get-tuple-element.31.key_t, bf16[3,4096,128]{2,1,0:T(8,128)(2,1)S(1)} %get-tuple-element.32.value, ...), custom_call_target="tpu_custom_call" | custom-call | flops 16000000000 | bytes 8000000 | tf_op jit(solution)/shard_map/pallas_call | solution.py:599
  100.3 1.2 %collective-permute-start.17 = (bf16[1664,128]{1,0:T(8,128)(2,1)S(1)}, bf16[1664,128]{1,0:T(8,128)(2,1)S(1)}, u32[]{:S(2)}, u32[]{:S(2)}) collective-permute-start(bf16[1664,128]{1,0:T(8,128)(2,1)S(1)} %get-tuple-element.34), channel_id=1, source_target_pairs={{0,24},{4,28},{8,0},{12,4},{16,8},{20,12},{24,16},{28,20},{32,56},... | collective-permute-start | bytes 1277960 | tf_op jit(solution)/shard_map/ppermute | solution.py:103
  101.5 0.9 collective-permute-start.18
  102.4 7.6 %shard_map.137.p0 = bf16[1664,128]{1,0:T(8,128)(2,1)S(1)} custom-call(s32[6]{0:T(128)S(1)} %pad_add_fusion.info_ref.band_ref, bf16[3,128,4096]{2,1,0:T(8,128)(2,1)S(1)} %get-tuple-element.31.key_t, bf16[3,4096,128]{2,1,0:T(8,128)(2,1)S(1)} %get-tuple-element.32.value, bf16[3,512,128]{2,1,0:T(8,128)(2,1)S(1)} %get-tuple-element.26.refs_0_, ...), custom_call_target="tpu_custom_call" | custom-call | flops 8000000000 | bytes 8000000 | tf_op jit(solution)/shard_map/pallas_call | solution.py:599
  110.1 1.9 %collective-permute-done.17.p1 = bf16[1664,128]{1,0:T(8,128)(2,1)S(1)} collective-permute-done((bf16[1664,128]{1,0:T(8,128)(2,1)S(1)}, bf16[1664,128]{1,0:T(8,128)(2,1)S(1)}, u32[]{:S(2)}, u32[]{:S(2)}) %collective-permute-start.17) | collective-permute-done | bytes 426016 | tf_op jit(solution)/shard_map/ppermute | solution.py:103
  112.0 2.0 %collective-permute-done.18.p2 = bf16[1664,128]{1,0:T(8,128)(2,1)S(1)} collective-permute-done((bf16[1664,128]{1,0:T(8,128)(2,1)S(1)}, bf16[1664,128]{1,0:T(8,128)(2,1)S(1)}, u32[]{:S(2)}, u32[]{:S(2)}) %collective-permute-start.18) | collective-permute-done | bytes 426016 | tf_op jit(solution)/shard_map/ppermute | solution.py:103
  114.0 1.9 %shard_map.139 = bf16[3,512,128]{2,1,0:T(8,128)(2,1)} custom-call(bf16[1664,128]{1,0:T(8,128)(2,1)S(1)} %shard_map.137.p0, bf16[1664,128]{1,0:T(8,128)(2,1)S(1)} %collective-permute-done.17.p1, bf16[1664,128]{1,0:T(8,128)(2,1)S(1)} %collective-permute-done.18.p2, bf16[1664,128]{1,0:T(8,128)(2,1)S(1)} %collective-permute-done.16.refs_1_.p3), custom_call_target="tpu_custom_call" | custom-call | tf_op jit(solution)/shard_map/pallas_call | solution.py:644
  (29 shorter events, 4.2 us)
Async XLA Ops:
  1.4 8.2 %collective-permute-start.1 = (bf16[2,1,8,512]{3,2,1,0:T(8,128)(2,1)S(1)}, bf16[2,1,8,512]{3,2,1,0:T(8,128)(2,1)S(1)}, u32[]{:S(2)}, u32[]{:S(2)}) collective-permute-start(bf16[2,1,8,512]{3,2,1,0:T(8,128)(2,1)S(1)} %get-tuple-element.36), channel_id=1, source_target_pairs={{1,0},{2,1},{3,2},{5,4},{6,5},{7,6},{9,8},{10,9},{11,10},{13,12},{... | collective-permute-start | bytes 49160 | tf_op jit(solution)/shard_map/ppermute | solution.py:117
  2.7 6.0 %collective-permute-start = (bf16[2,1,8,512]{3,2,1,0:T(8,128)(2,1)S(1)}, bf16[2,1,8,512]{3,2,1,0:T(8,128)(2,1)S(1)}, u32[]{:S(2)}, u32[]{:S(2)}) collective-permute-start(bf16[2,1,8,512]{3,2,1,0:T(8,128)(2,1)S(1)} %get-tuple-element.37), channel_id=1, source_target_pairs={{0,1},{1,2},{2,3},{4,5},{5,6},{6,7},{8,9},{9,10},{10,11},{12,13},{... | collective-permute-start | bytes 49160 | tf_op jit(solution)/shard_map/ppermute | solution.py:117
  9.6 8.7 %collective-permute-start.2 = (bf16[2,10,8,512]{3,2,1,0:T(8,128)(2,1)S(1)}, bf16[2,10,8,512]{3,2,1,0:T(8,128)(2,1)S(1)}, u32[]{:S(2)}, u32[]{:S(2)}) collective-permute-start(bf16[2,10,8,512]{3,2,1,0:T(8,128)(2,1)S(1)} %constant_dynamic-update-slice_fusion.cur_ref), channel_id=1, source_target_pairs={{0,4},{1,5},{2,6},{3,7},{4,8},{5,9},{6,10},{7,11},{8,12},{9,13},{1... | collective-permute-start | bytes 491528 | tf_op jit(solution)/shard_map/ppermute | solution.py:117
  18.3 11.9 %copy-start = (f32[3072]{0:T(1024)S(1)}, f32[3072]{0:T(1024)}, u32[]{:S(2)}) copy-start(f32[3072]{0:T(1024)} %param.18) | copy-start | bytes 36868
  18.3 11.9 %copy-start.1 = (f32[3072]{0:T(1024)S(1)}, f32[3072]{0:T(1024)}, u32[]{:S(2)}) copy-start(f32[3072]{0:T(1024)} %param.19) | copy-start | bytes 36868
  18.3 11.9 %copy-start.2 = (f32[3072]{0:T(1024)S(1)}, f32[3072]{0:T(1024)}, u32[]{:S(2)}) copy-start(f32[3072]{0:T(1024)} %param.20) | copy-start | bytes 36868
  18.3 11.9 %copy-start.3 = (f32[128]{0:T(128)S(1)}, f32[128]{0:T(128)}, u32[]{:S(2)}) copy-start(f32[128]{0:T(128)} %param.23) | copy-start | bytes 1540
  24.2 11.1 %collective-permute-start.5 = (bf16[144,512]{1,0:T(8,128)(2,1)S(1)}, bf16[144,512]{1,0:T(8,128)(2,1)S(1)}, u32[]{:S(2)}, u32[]{:S(2)}) collective-permute-start(bf16[144,512]{1,0:T(8,128)(2,1)S(1)} %get-tuple-element.22.s0), channel_id=1, source_target_pairs={{0,2},{1,3},{2,0},{3,1},{4,6},{5,7},{6,4},{7,5},{8,10},{9,11},{10,... | collective-permute-start | bytes 442376 | tf_op jit(solution)/shard_map/ppermute | solution.py:107
  28.2 8.5 %collective-permute-start.4 = (bf16[144,512]{1,0:T(8,128)(2,1)S(1)}, bf16[144,512]{1,0:T(8,128)(2,1)S(1)}, u32[]{:S(2)}, u32[]{:S(2)}) collective-permute-start(bf16[144,512]{1,0:T(8,128)(2,1)S(1)} %get-tuple-element.22.s0), channel_id=1, source_target_pairs={{0,3},{1,0},{2,1},{3,2},{4,7},{5,4},{6,5},{7,6},{8,11},{9,8},{10,9... | collective-permute-start | bytes 442376 | tf_op jit(solution)/shard_map/ppermute | solution.py:107
  29.2 7.8 %collective-permute-start.3 = (bf16[144,512]{1,0:T(8,128)(2,1)S(1)}, bf16[144,512]{1,0:T(8,128)(2,1)S(1)}, u32[]{:S(2)}, u32[]{:S(2)}) collective-permute-start(bf16[144,512]{1,0:T(8,128)(2,1)S(1)} %get-tuple-element.22.s0), channel_id=1, source_target_pairs={{0,1},{1,2},{2,3},{3,0},{4,5},{5,6},{6,7},{7,4},{8,9},{9,10},{10,1... | collective-permute-start | bytes 442376 | tf_op jit(solution)/shard_map/ppermute | solution.py:107
  38.1 11.2 %collective-permute-start.14 = (bf16[3,512,128]{2,1,0:T(8,128)(2,1)S(1)}, bf16[3,512,128]{2,1,0:T(8,128)(2,1)S(1)}, u32[]{:S(2)}, u32[]{:S(2)}) collective-permute-start(bf16[3,512,128]{2,1,0:T(8,128)(2,1)S(1)} %get-tuple-element.26.refs_0_), channel_id=1, source_target_pairs={{0,24},{4,28},{8,0},{12,4},{16,8},{20,12},{24,16},{28,20},{32,56},... | collective-permute-start | bytes 1179656 | tf_op jit(solution)/shard_map/ppermute | solution.py:103
  40.9 23.1 %collective-permute-start.12 = (bf16[528,512]{1,0:T(8,128)(2,1)S(1)}, bf16[528,512]{1,0:T(8,128)(2,1)S(1)}, u32[]{:S(2)}, u32[]{:S(2)}) collective-permute-start(bf16[528,512]{1,0:T(8,128)(2,1)S(1)} %get-tuple-element.27.a0), channel_id=1, source_target_pairs={{0,64},{4,68},{8,72},{12,76},{16,80},{20,84},{24,88},{28,92},{32,9... | collective-permute-start | bytes 1622024 | tf_op jit(solution)/shard_map/ppermute | solution.py:103
  42.3 23.7 %collective-permute-start.10 = (bf16[528,512]{1,0:T(8,128)(2,1)S(1)}, bf16[528,512]{1,0:T(8,128)(2,1)S(1)}, u32[]{:S(2)}, u32[]{:S(2)}) collective-permute-start(bf16[528,512]{1,0:T(8,128)(2,1)S(1)} %get-tuple-element.27.a0), channel_id=1, source_target_pairs={{0,96},{4,100},{8,104},{12,108},{16,112},{20,116},{24,120},{28,124... | collective-permute-start | bytes 1622024 | tf_op jit(solution)/shard_map/ppermute | solution.py:103
  44.1 22.6 %collective-permute-start.8 = (bf16[528,512]{1,0:T(8,128)(2,1)S(1)}, bf16[528,512]{1,0:T(8,128)(2,1)S(1)}, u32[]{:S(2)}, u32[]{:S(2)}) collective-permute-start(bf16[528,512]{1,0:T(8,128)(2,1)S(1)} %get-tuple-element.27.a0), channel_id=1, source_target_pairs={{0,32},{4,36},{8,40},{12,44},{16,48},{20,52},{24,56},{28,60},{32,6... | collective-permute-start | bytes 1622024 | tf_op jit(solution)/shard_map/ppermute | solution.py:103
  44.3 11.4 %collective-permute-start.13 = (bf16[3,512,128]{2,1,0:T(8,128)(2,1)S(1)}, bf16[3,512,128]{2,1,0:T(8,128)(2,1)S(1)}, u32[]{:S(2)}, u32[]{:S(2)}) collective-permute-start(bf16[3,512,128]{2,1,0:T(8,128)(2,1)S(1)} %get-tuple-element.26.refs_0_), channel_id=1, source_target_pairs={{0,8},{4,12},{8,16},{12,20},{16,24},{20,28},{24,0},{28,4},{32,40},... | collective-permute-start | bytes 1179656 | tf_op jit(solution)/shard_map/ppermute | solution.py:103
  49.3 14.6 %collective-permute-start.6 = (bf16[3,512,128]{2,1,0:T(8,128)(2,1)S(1)}, bf16[3,512,128]{2,1,0:T(8,128)(2,1)S(1)}, u32[]{:S(2)}, u32[]{:S(2)}) collective-permute-start(bf16[3,512,128]{2,1,0:T(8,128)(2,1)S(1)} %get-tuple-element.26.refs_0_), channel_id=1, source_target_pairs={{0,16},{4,20},{8,24},{12,28},{16,0},{20,4},{24,8},{28,12},{32,48},... | collective-permute-start | bytes 1179656 | tf_op jit(solution)/shard_map/ppermute | solution.py:103
  55.7 11.0 %collective-permute-start.7 = (bf16[528,512]{1,0:T(8,128)(2,1)S(1)}, bf16[528,512]{1,0:T(8,128)(2,1)S(1)}, u32[]{:S(2)}, u32[]{:S(2)}) collective-permute-start(bf16[528,512]{1,0:T(8,128)(2,1)S(1)} %get-tuple-element.27.a0), channel_id=1, source_target_pairs={{0,4},{4,0},{8,12},{12,8},{16,20},{20,16},{24,28},{28,24},{32,36},... | collective-permute-start | bytes 1622024 | tf_op jit(solution)/shard_map/ppermute | solution.py:103
  64.1 2.7 %collective-permute-start.15 = (bf16[528,512]{1,0:T(8,128)(2,1)S(1)}, bf16[528,512]{1,0:T(8,128)(2,1)S(1)}, u32[]{:S(2)}, u32[]{:S(2)}) collective-permute-start(bf16[528,512]{1,0:T(8,128)(2,1)S(1)} %shard_map.135.a2), channel_id=1, source_target_pairs={{0,4},{4,0},{8,12},{12,8},{16,20},{20,16},{24,28},{28,24},{32,36},... | collective-permute-start | bytes 1622024 | tf_op jit(solution)/shard_map/ppermute | solution.py:103
  66.0 1.9 %collective-permute-start.11 = (bf16[528,512]{1,0:T(8,128)(2,1)S(1)}, bf16[528,512]{1,0:T(8,128)(2,1)S(1)}, u32[]{:S(2)}, u32[]{:S(2)}) collective-permute-start(bf16[528,512]{1,0:T(8,128)(2,1)S(1)} %collective-permute-done.10.a3), channel_id=1, source_target_pairs={{0,4},{4,0},{8,12},{12,8},{16,20},{20,16},{24,28},{28,24},{32,36},... | collective-permute-start | bytes 1622024 | tf_op jit(solution)/shard_map/ppermute | solution.py:103
  66.7 2.0 %collective-permute-start.9 = (bf16[528,512]{1,0:T(8,128)(2,1)S(1)}, bf16[528,512]{1,0:T(8,128)(2,1)S(1)}, u32[]{:S(2)}, u32[]{:S(2)}) collective-permute-start(bf16[528,512]{1,0:T(8,128)(2,1)S(1)} %collective-permute-done.8.a1), channel_id=1, source_target_pairs={{0,4},{4,0},{8,12},{12,8},{16,20},{20,16},{24,28},{28,24},{32,36},... | collective-permute-start | bytes 1622024 | tf_op jit(solution)/shard_map/ppermute | solution.py:103
  82.4 20.0 %collective-permute-start.16 = (bf16[1664,128]{1,0:T(8,128)(2,1)S(1)}, bf16[1664,128]{1,0:T(8,128)(2,1)S(1)}, u32[]{:S(2)}, u32[]{:S(2)}) collective-permute-start(bf16[1664,128]{1,0:T(8,128)(2,1)S(1)} %get-tuple-element.33), channel_id=1, source_target_pairs={{0,16},{4,20},{8,24},{12,28},{16,0},{20,4},{24,8},{28,12},{32,48},... | collective-permute-start | bytes 1277960 | tf_op jit(solution)/shard_map/ppermute | solution.py:103
  100.3 11.7 %collective-permute-start.17 = (bf16[1664,128]{1,0:T(8,128)(2,1)S(1)}, bf16[1664,128]{1,0:T(8,128)(2,1)S(1)}, u32[]{:S(2)}, u32[]{:S(2)}) collective-permute-start(bf16[1664,128]{1,0:T(8,128)(2,1)S(1)} %get-tuple-element.34), channel_id=1, source_target_pairs={{0,24},{4,28},{8,0},{12,4},{16,8},{20,12},{24,16},{28,20},{32,56},... | collective-permute-start | bytes 1277960 | tf_op jit(solution)/shard_map/ppermute | solution.py:103
  101.5 12.5 %collective-permute-start.18 = (bf16[1664,128]{1,0:T(8,128)(2,1)S(1)}, bf16[1664,128]{1,0:T(8,128)(2,1)S(1)}, u32[]{:S(2)}, u32[]{:S(2)}) collective-permute-start(bf16[1664,128]{1,0:T(8,128)(2,1)S(1)} %get-tuple-element.35), channel_id=1, source_target_pairs={{0,8},{4,12},{8,16},{12,20},{16,24},{20,28},{24,0},{28,4},{32,40},... | collective-permute-start | bytes 1277960 | tf_op jit(solution)/shard_map/ppermute | solution.py:103
where the time goes:
time: 116 us
  Pallas kernels  55.4 us (48%)
  starting transfers between devices  28.6 us (25%)
  waiting for transfers between devices  28.1 us (24%)
  local copies, waits for them, and re-layouts  1.67 us (1%)
  other arithmetic  1.39 us (1%)
    ppermute x13, waiting for transfers between devices, shift_tm(): return lax.ppermute(block, 'tm', route)  24.9 us
    pallas_call x2, Pallas kernels, attend_next(): pl.pallas_call(functools.partial(next_kernel, groups), in_specs=[SMEM, VM...  22.4 us
    ppermute x13, starting transfers between devices, shift_tm(): return lax.ppermute(block, 'tm', route)  14.8 us
    pallas_call x1, Pallas kernels, attend_first(): pl.pallas_call(first_kernel, in_specs=[SMEM] + [ANY] * 13, out_specs=[VME...  13.7 us
    ppermute x3, starting transfers between devices, halo(): return lax.ppermute(block, ('tm', 'band'), route)  7.75 us
    ppermute x3, starting transfers between devices, shift_band(): return lax.ppermute(block, 'band', [(i, (i + db) % NB) for i in range(NB)])  6.02 us
    pallas_call x1, Pallas kernels, conv(): pl.pallas_call(conv_kernel, in_specs=[SMEM] + [VMEM] * 4 + [HBM] * 4, out...  5.81 us
    pallas_call x1, Pallas kernels, conv_newest(): pl.pallas_call(newest_kernel, in_specs=[VMEM] + [HBM] * 4, out_specs=[VME...  5.4 us
  transfers between devices with their start and end apart: 19, of which 13 were waited for; matrix products, arithmetic and copies ran while one was open for 2% of the time, Pallas kernels for 28%

commit v1 on v0

--- a/solution.py
+++ b/solution.py
@@ -333,31 +333,16 @@
     return (values * lax.rsqrt(mean_square + EPSILON) * gain).astype(BF16)
 
 
-def query_kernel(
-    band_ref, s0, s1, s3, s2, weight_ref, rows_ref, gain_ref, q_ref, xr_ref
-):
-    band = band_ref[5]
+def gather_rows(shards, first_row, band, out_ref):
     across = []
     sources = []
-    for back, ref in ((0, s0), (1, s1), (3, s3), (2, s2)):
+    for back, ref in zip((0, 1, 3, 2), shards):
         source = lax.rem(band + (NB - back), NB)
         sources.append(source)
-        cells = ref[0:SHARD, :]
-        extra = ref[SHARD : SHARD + 16, :].astype(F32)[0:1]
-        across.append(extra)
-        scale = jnp.transpose(jnp.broadcast_to(extra[:, 0:HD] + extra[:, HD : 2 * HD], (HD, HD)))
-        projected = (
-            jnp.dot(cells, weight_ref[...], preferred_element_type=F32) + rows_ref[0:1, 0:384]
-        )
-        for head in range(HEADS):
-            lanes = slice(head * HD, (head + 1) * HD)
-            values = normed(projected[:, lanes] * scale + rows_ref[1:2, lanes], gain_ref[...])
-            for i in range(2):
-                rows = pl.ds(pl.multiple_of(i * FRAME + source * 64, 64), 64)
-                q_ref[head, rows, :] = values[i * 64 : (i + 1) * 64]
+        across.append(ref[first_row + SHARD : first_row + SHARD + 16, :].astype(F32)[0:1])
         for i in range(2):
             rows = pl.ds(pl.multiple_of(i * FRAME + source * 64, 64), 64)
-            xr_ref[rows, :] = cells[i * 64 : (i + 1) * 64]
+            out_ref[rows, :] = ref[first_row + i * 64 : first_row + (i + 1) * 64, :]
     lines = []
     for term in range(2):
         pieces = []
@@ -371,23 +356,46 @@
         lines.append(jnp.concatenate(pieces, axis=1))
     place = lax.broadcasted_iota(jnp.int32, (16, 512), 0)
     tail = jnp.where(place == 0, lines[0], jnp.where(place == 1, lines[1], 0.0))
-    xr_ref[OWN : OWN + 16, :] = tail.astype(BF16)
-
-
-def queries_of(band, shards, weight, rows, gain):
+    out_ref[OWN : OWN + 16, :] = tail.astype(BF16)
+    return sources, across
+
+
+def query_kernel(
+    band_ref, s0, s1, s3, s2, x_near, x_far, weight_ref, rows_ref, gain_ref, q_ref, xr_ref, pair_ref
+):
+    shards = (s0, s1, s3, s2)
+    pair_ref[0 : SHARD + 16, :] = x_near[...]
+    pair_ref[SHARD + 16 : 2 * (SHARD + 16), :] = x_far[...]
+    sources, across = gather_rows(shards, 0, band_ref[5], xr_ref)
+    for ref, source, extra in zip(shards, sources, across):
+        scale = jnp.transpose(jnp.broadcast_to(extra[:, 0:HD] + extra[:, HD : 2 * HD], (HD, HD)))
+        projected = (
+            jnp.dot(ref[0:SHARD, :], weight_ref[...], preferred_element_type=F32)
+            + rows_ref[0:1, 0:384]
+        )
+        for head in range(HEADS):
+            lanes = slice(head * HD, (head + 1) * HD)
+            values = normed(projected[:, lanes] * scale + rows_ref[1:2, lanes], gain_ref[...])
+            for i in range(2):
+                rows = pl.ds(pl.multiple_of(i * FRAME + source * 64, 64), 64)
+                q_ref[head, rows, :] = values[i * 64 : (i + 1) * 64]
+
+
+def queries_of(info, shards, across, weight, rows, gain):
     return pl.pallas_call(
         query_kernel,
-        in_specs=[SMEM] + [VMEM] * 7,
-        out_specs=[VMEM, VMEM],
+        in_specs=[SMEM] + [VMEM] * 9,
+        out_specs=[VMEM] * 3,
         out_shape=[
             jax.ShapeDtypeStruct((HEADS, OWN, HD), BF16),
             jax.ShapeDtypeStruct((OWN + 16, 512), BF16),
+            jax.ShapeDtypeStruct((2 * (SHARD + 16), 512), BF16),
         ],
         compiler_params=params(8),
         cost_estimate=pl.CostEstimate(
             flops=2 * 512 * 512 * 384, bytes_accessed=2000000, transcendentals=0
         ),
-    )(band, *in_vmem(*shards, weight, rows), gain[None] * FACTOR)
+    )(info, *in_vmem(*shards, *across, weight, rows), gain[None] * FACTOR)
 
 
 def store_rows(o_ref, base, results):
@@ -508,28 +516,38 @@
 
 
 def first_kernel(
-    info_ref, q_hbm, a0, b0, a1, b1, a3, b3, a2, b2, wk_hbm, wv_hbm, rows_hbm, cols_hbm,
-    o2, key_out, value_out, key_t, value, blocks, q2, wk_ref, wv_ref, rows_ref, cols_ref,
+    info_ref, q_hbm, a0, b0, a1, b1, a3, b3, g0, g1, g3, g2, wk_hbm, wv_hbm, rows_hbm, cols_hbm,
+    o2, key_out, value_out, key_t, value, blocks, pairs, q2, wk_ref, wv_ref, rows_ref, cols_ref,
     sems,
 ):
     x_here, _, core = place_of(info_ref)
     weight_copies = fetch(
         (wk_hbm, wv_hbm, rows_hbm, cols_hbm), (wk_ref, wv_ref, rows_ref, cols_ref), sems
     )
-    sources = (a0, b0, a1, b1, a3, b3, a2, b2)
-    block_copies = fetch(sources, [blocks.at[i] for i in range(8)], sems, 4)
-    (query_copy,) = fetch([q_hbm], [q2], sems, 12)
+    block_copies = fetch((a0, b0, a1, b1, a3, b3), [blocks.at[i] for i in range(6)], sems, 4)
+    pair_copies = fetch((g0, g1, g3, g2), [pairs.at[i] for i in range(4)], sems, 10)
+    (query_copy,) = fetch([q_hbm], [q2], sems, 14)
     for copy in weight_copies:
         copy.wait()
     for at in range(8):
-        if at % 4 == 0:
-            for copy in block_copies[at : at + 4]:
+        if at == 0:
+            for copy in block_copies:
                 copy.wait()
+        if at == 4:
+            for copy in pair_copies:
+                copy.wait()
+            for swap in range(2):
+                gather_rows(
+                    [pairs.at[i] for i in range(4)],
+                    swap * (SHARD + 16),
+                    info_ref[5],
+                    blocks.at[6 + swap],
+                )
         source = lax.rem(x_here + (NX - (0, 1, 3, 2)[at // 2]), NX)
         core_at = core if at % 2 == 0 else 1 - core
         start = pl.multiple_of((source * 2 + core_at) * OWN, OWN)
         project_block(blocks.at[at], start, wk_ref, wv_ref, rows_ref, cols_ref, key_t, value)
-    copies = fetch((key_t, value), (key_out, value_out), sems, 13)
+    copies = fetch((key_t, value), (key_out, value_out), sems, 15)
     query_copy.wait()
     attend_group(info_ref, 2, q2, o2, key_t, value)
     for copy in copies:
@@ -539,10 +557,10 @@
 PARTIAL = jax.ShapeDtypeStruct((HEADS * OWN + 128, HD), BF16)
 
 
-def attend_first(info, query, near, far, wk, wv, rows, cols):
+def attend_first(info, query, near, far, pairs, wk, wv, rows, cols):
     return pl.pallas_call(
         first_kernel,
-        in_specs=[SMEM] + [ANY] * 13,
+        in_specs=[SMEM] + [ANY] * 15,
         out_specs=[VMEM, ANY, ANY],
         out_shape=[
             PARTIAL,
@@ -553,12 +571,13 @@
             pltpu.VMEM((HEADS, HD, KEYS), BF16),
             pltpu.VMEM((HEADS, KEYS, HD), BF16),
             pltpu.VMEM((8, OWN + 16, 512), BF16),
+            pltpu.VMEM((4, 2 * (SHARD + 16), 512), BF16),
             pltpu.VMEM((HEADS, OWN, HD), BF16),
             pltpu.VMEM((384, 512), BF16),
             pltpu.VMEM((512, 384), BF16),
             pltpu.VMEM((8, 1152), F32),
             pltpu.VMEM((3, 384, HD), F32),
-            pltpu.SemaphoreType.DMA((15,)),
+            pltpu.SemaphoreType.DMA((17,)),
         ],
         compiler_params=params(34),
         cost_estimate=pl.CostEstimate(
@@ -568,6 +587,7 @@
         info,
         query,
         *[block for pair in zip(near, far) for block in pair],
+        *pairs,
         wk,
         wv,
         rows,
@@ -680,16 +700,16 @@
         embed_near, embed_bias, mod_shift, mod_scale, k_gain, qkv_near
     )
     shards = (send, shift_band(send, 1), shift_band(send, 3), shift_band(send, 2))
-    query, xr = queries_of(
-        info, shards, wq, rows, q_gain
-    )
+    across = (shift_tm(send, dx=2), shift_tm(send, dx=2, swap=True))
+    query, xr, pair = queries_of(info, shards, across, wq, rows, q_gain)
     far_own = shift_tm(xr, swap=True)
-    a1, a3 = shift_tm(xr, dx=1), shift_tm(xr, dx=3)
     q1, q3, q2 = shift_tm(query, dz=1), shift_tm(query, dz=3), shift_tm(query, dz=2)
-    a2 = after(shift_tm(xr, dx=2), q1, q3, q2)
-    near = (xr, a1, a3, a2)
-    far = (far_own,) + tuple(shift_tm(part, swap=True) for part in near[1:])
-    o2, key_t, value = attend_first(info, q2, near, far, wk, wv, rows, cols)
+    pairs = (pair, shift_band(pair, 1), shift_band(pair, 3), shift_band(pair, 2))
+    a1 = after(shift_tm(xr, dx=1), q2, pairs[3])
+    a3 = after(shift_tm(xr, dx=3), pairs[1], pairs[2])
+    near = (xr, a1, a3)
+    far = (far_own, shift_tm(a1, swap=True), shift_tm(a3, swap=True))
+    o2, key_t, value = attend_first(info, q2, near, far, pairs, wk, wv, rows, cols)
     p2 = shift_tm(o2, dz=2)
     o1, o3 = attend_next((1, 3), info, (q1, q3), key_t, value)
     p1, p3 = shift_tm(o1, dz=3), shift_tm(o3, dz=1)

time: 116 us -> 111 us (0.957)
  waiting for transfers between devices: 28.1 us -> 18.6 us
  starting transfers between devices: 28.6 us -> 32.7 us
    ppermute x13, waiting for transfers between devices: 24.9 us -> 9.95 us  [shift_tm(): return lax.ppermute(block, 'tm', route)]
    ppermute x3 -> x6, waiting for transfers between devices: 1.77 us -> 5.19 us  [shift_band(): return lax.ppermute(block, 'band', [(i, (i + db) % NB) for i in range(NB)])]
    ppermute x13, starting transfers between devices: 14.8 us -> 18.2 us  [shift_tm(): return lax.ppermute(block, 'tm', route)]
    ppermute x3, waiting for transfers between devices: 1.44 us -> 3.42 us  [halo(): return lax.ppermute(block, ('tm', 'band'), route)]
    ppermute x3 -> x6, starting transfers between devices: 6.02 us -> 7.86 us  [shift_band(): return lax.ppermute(block, 'band', [(i, (i + db) % NB) for i in range(NB)])]
  transfers between devices with their start and end apart: 19 -> 22, of which waited for: 13 -> 9; matrix products, arithmetic and copies ran while one was open for 2% -> 2% of each run, Pallas kernels for 28% -> 42%
where the time goes in v1:
time: 111 us
  Pallas kernels  55.9 us (50%)
  starting transfers between devices  32.7 us (29%)
  waiting for transfers between devices  18.6 us (17%)
  local copies, waits for them, and re-layouts  1.67 us (2%)
  other arithmetic  1.39 us (1%)
    pallas_call x2, Pallas kernels, attend_next(): pl.pallas_call(functools.partial(next_kernel, groups), in_specs=[SMEM, VM...  22.4 us
    ppermute x13, starting transfers between devices, shift_tm(): return lax.ppermute(block, 'tm', route)  18.2 us
    pallas_call x1, Pallas kernels, attend_first(): pl.pallas_call(first_kernel, in_specs=[SMEM] + [ANY] * 15, out_specs=[VME...  14 us
    ppermute x13, waiting for transfers between devices, shift_tm(): return lax.ppermute(block, 'tm', route)  9.95 us
    ppermute x6, starting transfers between devices, shift_band(): return lax.ppermute(block, 'band', [(i, (i + db) % NB) for i in range(NB)])  7.86 us
    ppermute x3, starting transfers between devices, halo(): return lax.ppermute(block, ('tm', 'band'), route)  6.67 us
    pallas_call x1, Pallas kernels, conv(): pl.pallas_call(conv_kernel, in_specs=[SMEM] + [VMEM] * 4 + [HBM] * 4, out...  5.82 us
    pallas_call x1, Pallas kernels, conv_newest(): pl.pallas_call(newest_kernel, in_specs=[VMEM] + [HBM] * 4, out_specs=[VME...  5.4 us
  transfers between devices with their start and end apart: 22, of which 9 were waited for; matrix products, arithmetic and copies ran while one was open for 2% of the time, Pallas kernels for 42%

profile of v1, /device:TPU:2, one launch (start us, length us, event | category | flops | bytes accessed | tf_op | source)
XLA Modules:
  0.0 111.0 jit_solution(3723703550614466048)
XLA Ops:
  0.6 0.7 fusion
  1.4 3.5 %collective-permute-start = (bf16[2,1,8,512]{3,2,1,0:T(8,128)(2,1)S(1)}, bf16[2,1,8,512]{3,2,1,0:T(8,128)(2,1)S(1)}, u32[]{:S(2)}, u32[]{:S(2)}) collective-permute-start(bf16[2,1,8,512]{3,2,1,0:T(8,128)(2,1)S(1)} %get-tuple-element.39), channel_id=1, source_target_pairs={{0,1},{1,2},{2,3},{4,5},{5,6},{6,7},{8,9},{9,10},{10,11},{12,13},{... | collective-permute-start | bytes 49160 | tf_op jit(solution)/shard_map/ppermute | solution.py:117
  4.8 1.3 %collective-permute-start.1 = (bf16[2,1,8,512]{3,2,1,0:T(8,128)(2,1)S(1)}, bf16[2,1,8,512]{3,2,1,0:T(8,128)(2,1)S(1)}, u32[]{:S(2)}, u32[]{:S(2)}) collective-permute-start(bf16[2,1,8,512]{3,2,1,0:T(8,128)(2,1)S(1)} %get-tuple-element.38), channel_id=1, source_target_pairs={{1,0},{2,1},{3,2},{5,4},{6,5},{7,6},{9,8},{10,9},{11,10},{13,12},{... | collective-permute-start | bytes 49160 | tf_op jit(solution)/shard_map/ppermute | solution.py:117
  6.8 0.9 constant_dynamic-update-slice_fusion.1
  7.7 2.7 %collective-permute-done.1 = bf16[2,1,8,512]{3,2,1,0:T(8,128)(2,1)S(1)} collective-permute-done((bf16[2,1,8,512]{3,2,1,0:T(8,128)(2,1)S(1)}, bf16[2,1,8,512]{3,2,1,0:T(8,128)(2,1)S(1)}, u32[]{:S(2)}, u32[]{:S(2)}) %collective-permute-start.1) | collective-permute-done | bytes 16416 | tf_op jit(solution)/shard_map/ppermute | solution.py:117
  10.5 1.9 %collective-permute-start.2 = (bf16[2,10,8,512]{3,2,1,0:T(8,128)(2,1)S(1)}, bf16[2,10,8,512]{3,2,1,0:T(8,128)(2,1)S(1)}, u32[]{:S(2)}, u32[]{:S(2)}) collective-permute-start(bf16[2,10,8,512]{3,2,1,0:T(8,128)(2,1)S(1)} %constant_dynamic-update-slice_fusion.cur_ref), channel_id=1, source_target_pairs={{0,4},{1,5},{2,6},{3,7},{4,8},{5,9},{6,10},{7,11},{8,12},{9,13},{1... | collective-permute-start | bytes 491528 | tf_op jit(solution)/shard_map/ppermute | solution.py:117
  13.1 5.4 %shard_map.131 = (f32[128,512]{1,0:T(8,128)S(1)}, bf16[512,3072]{1,0:T(8,128)(2,1)S(1)}, bf16[9,3072,128]{2,1,0:T(8,128)(2,1)S(1)}) custom-call(bf16[2,10,8,512]{3,2,1,0:T(8,128)(2,1)S(1)} %constant_dynamic-update-slice_fusion.cur_ref, f32[1,512]{1,0:T(1,128)} %bitcast.21, bf16[3,3,3,512,512]{4,3,2,1,0:T(8,128)(2,1)} %weight_hbm.3, ...), custom_call_target="tpu_custom_call" | custom-call | flops 603979776 | bytes 15000000 | tf_op jit(solution)/shard_map/pallas_call | solution.py:225
  19.2 5.8 %shard_map.132 = (bf16[2,8,8,512]{3,2,1,0:T(8,128)(2,1)}, bf16[144,512]{1,0:T(8,128)(2,1)S(1)}) custom-call(s32[6]{0:T(128)S(1)} %pad_add_fusion.info_ref.band_ref, bf16[2,10,8,512]{3,2,1,0:T(8,128)(2,1)S(1)} %constant_dynamic-update-slice_fusion.cur_ref, bf16[2,10,8,512]{3,2,1,0:T(8,128)(2,1)S(1)} %collective-permute-done.2.prev_ref, ...), custom_call_target="tpu_custom_call" | custom-call | flops 1811939328 | bytes 12000000 | tf_op jit(solution)/shard_map/pallas_call | solution.py:304
  25.1 1.6 %collective-permute-start.3 = (bf16[144,512]{1,0:T(8,128)(2,1)S(1)}, bf16[144,512]{1,0:T(8,128)(2,1)S(1)}, u32[]{:S(2)}, u32[]{:S(2)}) collective-permute-start(bf16[144,512]{1,0:T(8,128)(2,1)S(1)} %get-tuple-element.23.s0), channel_id=1, source_target_pairs={{0,1},{1,2},{2,3},{3,0},{4,5},{5,6},{6,7},{7,4},{8,9},{9,10},{10,1... | collective-permute-start | bytes 442376 | tf_op jit(solution)/shard_map/ppermute | solution.py:107
  26.7 1.7 %collective-permute-start.4 = (bf16[144,512]{1,0:T(8,128)(2,1)S(1)}, bf16[144,512]{1,0:T(8,128)(2,1)S(1)}, u32[]{:S(2)}, u32[]{:S(2)}) collective-permute-start(bf16[144,512]{1,0:T(8,128)(2,1)S(1)} %get-tuple-element.23.s0), channel_id=1, source_target_pairs={{0,3},{1,0},{2,1},{3,2},{4,7},{5,4},{6,5},{7,6},{8,11},{9,8},{10,9... | collective-permute-start | bytes 442376 | tf_op jit(solution)/shard_map/ppermute | solution.py:107
  28.4 1.7 %collective-permute-start.5 = (bf16[144,512]{1,0:T(8,128)(2,1)S(1)}, bf16[144,512]{1,0:T(8,128)(2,1)S(1)}, u32[]{:S(2)}, u32[]{:S(2)}) collective-permute-start(bf16[144,512]{1,0:T(8,128)(2,1)S(1)} %get-tuple-element.23.s0), channel_id=1, source_target_pairs={{0,2},{1,3},{2,0},{3,1},{4,6},{5,7},{6,4},{7,5},{8,10},{9,11},{10,... | collective-permute-start | bytes 442376 | tf_op jit(solution)/shard_map/ppermute | solution.py:107
  30.1 2.1 %collective-permute-start.6 = (bf16[144,512]{1,0:T(8,128)(2,1)S(1)}, bf16[144,512]{1,0:T(8,128)(2,1)S(1)}, u32[]{:S(2)}, u32[]{:S(2)}) collective-permute-start(bf16[144,512]{1,0:T(8,128)(2,1)S(1)} %get-tuple-element.23.s0), channel_id=1, source_target_pairs={{0,64},{4,68},{8,72},{12,76},{16,80},{20,84},{24,88},{28,92},{32,9... | collective-permute-start | bytes 442376 | tf_op jit(solution)/shard_map/ppermute | solution.py:103
  32.2 1.3 %collective-permute-start.7 = (bf16[144,512]{1,0:T(8,128)(2,1)S(1)}, bf16[144,512]{1,0:T(8,128)(2,1)S(1)}, u32[]{:S(2)}, u32[]{:S(2)}) collective-permute-start(bf16[144,512]{1,0:T(8,128)(2,1)S(1)} %get-tuple-element.23.s0), channel_id=1, source_target_pairs={{0,68},{4,64},{8,76},{12,72},{16,84},{20,80},{24,92},{28,88},{32,1... | collective-permute-start | bytes 442376 | tf_op jit(solution)/shard_map/ppermute | solution.py:103
  33.5 5.0 %shard_map.133 = (bf16[512,384]{1,0:T(8,128)(2,1)S(1)}, bf16[384,512]{1,0:T(8,128)(2,1)S(1)}, bf16[512,384]{1,0:T(8,128)(2,1)S(1)}, f32[8,1152]{1,0:T(8,128)S(1)}, f32[3,384,128]{2,1,0:T(8,128)S(1)}) custom-call(bf16[512,3072]{1,0:T(8,128)(2,1)S(1)} %get-tuple-element.21.embed_ref, f32[1,3072]{1,0:T(1,128)S(1)} %bitcast.15, f32[1,3072]{1,0:T(1,128)S(1)} %bitcast.16, ...), custom_call_target="tpu_custom_call" | custom-call | flops 3737124864 | bytes 12000000 | tf_op jit(solution)/shard_map/pallas_call | solution.py:161
  38.5 2.1 %collective-permute-done.7.x_far = bf16[144,512]{1,0:T(8,128)(2,1)S(1)} collective-permute-done((bf16[144,512]{1,0:T(8,128)(2,1)S(1)}, bf16[144,512]{1,0:T(8,128)(2,1)S(1)}, u32[]{:S(2)}, u32[]{:S(2)}) %collective-permute-start.7) | collective-permute-done | bytes 147488 | tf_op jit(solution)/shard_map/ppermute | solution.py:103
  40.7 1.2 %shard_map.134 = (bf16[3,512,128]{2,1,0:T(8,128)(2,1)S(1)}, bf16[528,512]{1,0:T(8,128)(2,1)S(1)}, bf16[288,512]{1,0:T(8,128)(2,1)S(1)}) custom-call(s32[6]{0:T(128)S(1)} %pad_add_fusion.info_ref.band_ref, bf16[144,512]{1,0:T(8,128)(2,1)S(1)} %get-tuple-element.23.s0, bf16[144,512]{1,0:T(8,128)(2,1)S(1)} %collective-permute-done.3.s1, ...), custom_call_target="tpu_custom_call" | custom-call | flops 201326592 | bytes 2000000 | tf_op jit(solution)/shard_map/pallas_call | solution.py:385
  41.9 1.9 %collective-permute-start.11 = (bf16[288,512]{1,0:T(8,128)(2,1)S(1)}, bf16[288,512]{1,0:T(8,128)(2,1)S(1)}, u32[]{:S(2)}, u32[]{:S(2)}) collective-permute-start(bf16[288,512]{1,0:T(8,128)(2,1)S(1)} %get-tuple-element.29.g0), channel_id=1, source_target_pairs={{0,2},{1,3},{2,0},{3,1},{4,6},{5,7},{6,4},{7,5},{8,10},{9,11},{10,... | collective-permute-start | bytes 884744 | tf_op jit(solution)/shard_map/ppermute | solution.py:107
  43.8 1.5 %collective-permute-start.10 = (bf16[528,512]{1,0:T(8,128)(2,1)S(1)}, bf16[528,512]{1,0:T(8,128)(2,1)S(1)}, u32[]{:S(2)}, u32[]{:S(2)}) collective-permute-start(bf16[528,512]{1,0:T(8,128)(2,1)S(1)} %get-tuple-element.28.a0), channel_id=1, source_target_pairs={{0,32},{4,36},{8,40},{12,44},{16,48},{20,52},{24,56},{28,60},{32,6... | collective-permute-start | bytes 1622024 | tf_op jit(solution)/shard_map/ppermute | solution.py:103
  45.8 3.8 %collective-permute-start.8 = (bf16[3,512,128]{2,1,0:T(8,128)(2,1)S(1)}, bf16[3,512,128]{2,1,0:T(8,128)(2,1)S(1)}, u32[]{:S(2)}, u32[]{:S(2)}) collective-permute-start(bf16[3,512,128]{2,1,0:T(8,128)(2,1)S(1)} %get-tuple-element.27.refs_0_), channel_id=1, source_target_pairs={{0,16},{4,20},{8,24},{12,28},{16,0},{20,4},{24,8},{28,12},{32,48},... | collective-permute-start | bytes 1179656 | tf_op jit(solution)/shard_map/ppermute | solution.py:103
  50.0 3.3 %collective-permute-done.11.refs_1_.g2 = bf16[288,512]{1,0:T(8,128)(2,1)S(1)} collective-permute-done((bf16[288,512]{1,0:T(8,128)(2,1)S(1)}, bf16[288,512]{1,0:T(8,128)(2,1)S(1)}, u32[]{:S(2)}, u32[]{:S(2)}) %collective-permute-start.11) | collective-permute-done | bytes 294944 | tf_op jit(solution)/shard_map/ppermute | solution.py:107
  53.9 4.3 %collective-permute-done.8.refs_0_.q_hbm = bf16[3,512,128]{2,1,0:T(8,128)(2,1)S(1)} collective-permute-done((bf16[3,512,128]{2,1,0:T(8,128)(2,1)S(1)}, bf16[3,512,128]{2,1,0:T(8,128)(2,1)S(1)}, u32[]{:S(2)}, u32[]{:S(2)}) %collective-permute-start.8) | collective-permute-done | bytes 393248 | tf_op jit(solution)/shard_map/ppermute | solution.py:103
  59.2 1.6 %collective-permute-done.15.refs_1_.g3 = bf16[288,512]{1,0:T(8,128)(2,1)S(1)} collective-permute-done((bf16[288,512]{1,0:T(8,128)(2,1)S(1)}, bf16[288,512]{1,0:T(8,128)(2,1)S(1)}, u32[]{:S(2)}, u32[]{:S(2)}) %collective-permute-start.15) | collective-permute-done | bytes 294944 | tf_op jit(solution)/shard_map/ppermute | solution.py:107
  60.9 1.5 %collective-permute-start.18 = (bf16[3,512,128]{2,1,0:T(8,128)(2,1)S(1)}, bf16[3,512,128]{2,1,0:T(8,128)(2,1)S(1)}, u32[]{:S(2)}, u32[]{:S(2)}) collective-permute-start(bf16[3,512,128]{2,1,0:T(8,128)(2,1)S(1)} %get-tuple-element.27.refs_0_), channel_id=1, source_target_pairs={{0,8},{4,12},{8,16},{12,20},{16,24},{20,28},{24,0},{28,4},{32,40},... | collective-permute-start | bytes 1179656 | tf_op jit(solution)/shard_map/ppermute | solution.py:103
  62.5 1.8 %collective-permute-start.19 = (bf16[3,512,128]{2,1,0:T(8,128)(2,1)S(1)}, bf16[3,512,128]{2,1,0:T(8,128)(2,1)S(1)}, u32[]{:S(2)}, u32[]{:S(2)}) collective-permute-start(bf16[3,512,128]{2,1,0:T(8,128)(2,1)S(1)} %get-tuple-element.27.refs_0_), channel_id=1, source_target_pairs={{0,24},{4,28},{8,0},{12,4},{16,8},{20,12},{24,16},{28,20},{32,56},... | collective-permute-start | bytes 1179656 | tf_op jit(solution)/shard_map/ppermute | solution.py:103
  64.2 14.0 %shard_map.137 = (bf16[1664,128]{1,0:T(8,128)(2,1)S(1)}, bf16[3,128,4096]{2,1,0:T(8,128)(2,1)S(1)}, bf16[3,4096,128]{2,1,0:T(8,128)(2,1)S(1)}) custom-call(s32[6]{0:T(128)S(1)} %pad_add_fusion.info_ref.band_ref, bf16[3,512,128]{2,1,0:T(8,128)(2,1)S(1)} %collective-permute-done.8.refs_0_.q_hbm, bf16[528,512]{1,0:T(8,128)(2,1)S(1)} %get-tuple-element.28.a0, ...), custom_call_target="tpu_custom_call" | custom-call | flops 15000000512 | bytes 10000000 | tf_op jit(solution)/shard_map/pallas_call | solution.py:561
  78.3 2.9 %collective-permute-start.17 = (bf16[1664,128]{1,0:T(8,128)(2,1)S(1)}, bf16[1664,128]{1,0:T(8,128)(2,1)S(1)}, u32[]{:S(2)}, u32[]{:S(2)}) collective-permute-start(bf16[1664,128]{1,0:T(8,128)(2,1)S(1)} %get-tuple-element.35), channel_id=1, source_target_pairs={{0,16},{4,20},{8,24},{12,28},{16,0},{20,4},{24,8},{28,12},{32,48},... | collective-permute-start | bytes 1277960 | tf_op jit(solution)/shard_map/ppermute | solution.py:103
  81.2 14.7 %shard_map.139 = (bf16[1664,128]{1,0:T(8,128)(2,1)S(1)}, bf16[1664,128]{1,0:T(8,128)(2,1)S(1)}) custom-call(s32[6]{0:T(128)S(1)} %pad_add_fusion.info_ref.band_ref, bf16[3,128,4096]{2,1,0:T(8,128)(2,1)S(1)} %get-tuple-element.33.key_t, bf16[3,4096,128]{2,1,0:T(8,128)(2,1)S(1)} %get-tuple-element.34.value, ...), custom_call_target="tpu_custom_call" | custom-call | flops 16000000000 | bytes 8000000 | tf_op jit(solution)/shard_map/pallas_call | solution.py:619
  96.6 1.4 %collective-permute-start.21 = (bf16[1664,128]{1,0:T(8,128)(2,1)S(1)}, bf16[1664,128]{1,0:T(8,128)(2,1)S(1)}, u32[]{:S(2)}, u32[]{:S(2)}) collective-permute-start(bf16[1664,128]{1,0:T(8,128)(2,1)S(1)} %get-tuple-element.37), channel_id=1, source_target_pairs={{0,8},{4,12},{8,16},{12,20},{16,24},{20,28},{24,0},{28,4},{32,40},... | collective-permute-start | bytes 1277960 | tf_op jit(solution)/shard_map/ppermute | solution.py:103
  98.0 7.6 %shard_map.138.p0 = bf16[1664,128]{1,0:T(8,128)(2,1)S(1)} custom-call(s32[6]{0:T(128)S(1)} %pad_add_fusion.info_ref.band_ref, bf16[3,128,4096]{2,1,0:T(8,128)(2,1)S(1)} %get-tuple-element.33.key_t, bf16[3,4096,128]{2,1,0:T(8,128)(2,1)S(1)} %get-tuple-element.34.value, bf16[3,512,128]{2,1,0:T(8,128)(2,1)S(1)} %get-tuple-element.27.refs_0_, ...), custom_call_target="tpu_custom_call" | custom-call | flops 8000000000 | bytes 8000000 | tf_op jit(solution)/shard_map/pallas_call | solution.py:619
  105.6 1.7 %collective-permute-done.20.p1 = bf16[1664,128]{1,0:T(8,128)(2,1)S(1)} collective-permute-done((bf16[1664,128]{1,0:T(8,128)(2,1)S(1)}, bf16[1664,128]{1,0:T(8,128)(2,1)S(1)}, u32[]{:S(2)}, u32[]{:S(2)}) %collective-permute-start.20) | collective-permute-done | bytes 426016 | tf_op jit(solution)/shard_map/ppermute | solution.py:103
  107.3 1.8 %collective-permute-done.21.p2 = bf16[1664,128]{1,0:T(8,128)(2,1)S(1)} collective-permute-done((bf16[1664,128]{1,0:T(8,128)(2,1)S(1)}, bf16[1664,128]{1,0:T(8,128)(2,1)S(1)}, u32[]{:S(2)}, u32[]{:S(2)}) %collective-permute-start.21) | collective-permute-done | bytes 426016 | tf_op jit(solution)/shard_map/ppermute | solution.py:103
  109.1 1.9 %shard_map.140 = bf16[3,512,128]{2,1,0:T(8,128)(2,1)} custom-call(bf16[1664,128]{1,0:T(8,128)(2,1)S(1)} %shard_map.138.p0, bf16[1664,128]{1,0:T(8,128)(2,1)S(1)} %collective-permute-done.20.p1, bf16[1664,128]{1,0:T(8,128)(2,1)S(1)} %collective-permute-done.21.p2, bf16[1664,128]{1,0:T(8,128)(2,1)S(1)} %collective-permute-done.17.refs_1_.p3), custom_call_target="tpu_custom_call" | custom-call | tf_op jit(solution)/shard_map/pallas_call | solution.py:664
  (36 shorter events, 5.4 us)
Async XLA Ops:
  1.4 5.4 %collective-permute-start = (bf16[2,1,8,512]{3,2,1,0:T(8,128)(2,1)S(1)}, bf16[2,1,8,512]{3,2,1,0:T(8,128)(2,1)S(1)}, u32[]{:S(2)}, u32[]{:S(2)}) collective-permute-start(bf16[2,1,8,512]{3,2,1,0:T(8,128)(2,1)S(1)} %get-tuple-element.39), channel_id=1, source_target_pairs={{0,1},{1,2},{2,3},{4,5},{5,6},{6,7},{8,9},{9,10},{10,11},{12,13},{... | collective-permute-start | bytes 49160 | tf_op jit(solution)/shard_map/ppermute | solution.py:117
  4.8 5.6 %collective-permute-start.1 = (bf16[2,1,8,512]{3,2,1,0:T(8,128)(2,1)S(1)}, bf16[2,1,8,512]{3,2,1,0:T(8,128)(2,1)S(1)}, u32[]{:S(2)}, u32[]{:S(2)}) collective-permute-start(bf16[2,1,8,512]{3,2,1,0:T(8,128)(2,1)S(1)} %get-tuple-element.38), channel_id=1, source_target_pairs={{1,0},{2,1},{3,2},{5,4},{6,5},{7,6},{9,8},{10,9},{11,10},{13,12},{... | collective-permute-start | bytes 49160 | tf_op jit(solution)/shard_map/ppermute | solution.py:117
  10.5 8.7 %collective-permute-start.2 = (bf16[2,10,8,512]{3,2,1,0:T(8,128)(2,1)S(1)}, bf16[2,10,8,512]{3,2,1,0:T(8,128)(2,1)S(1)}, u32[]{:S(2)}, u32[]{:S(2)}) collective-permute-start(bf16[2,10,8,512]{3,2,1,0:T(8,128)(2,1)S(1)} %constant_dynamic-update-slice_fusion.cur_ref), channel_id=1, source_target_pairs={{0,4},{1,5},{2,6},{3,7},{4,8},{5,9},{6,10},{7,11},{8,12},{9,13},{1... | collective-permute-start | bytes 491528 | tf_op jit(solution)/shard_map/ppermute | solution.py:117
  19.2 14.2 %copy-start = (f32[3072]{0:T(1024)S(1)}, f32[3072]{0:T(1024)}, u32[]{:S(2)}) copy-start(f32[3072]{0:T(1024)} %param.18) | copy-start | bytes 36868
  19.2 14.2 %copy-start.1 = (f32[3072]{0:T(1024)S(1)}, f32[3072]{0:T(1024)}, u32[]{:S(2)}) copy-start(f32[3072]{0:T(1024)} %param.19) | copy-start | bytes 36868
  19.2 14.2 %copy-start.2 = (f32[3072]{0:T(1024)S(1)}, f32[3072]{0:T(1024)}, u32[]{:S(2)}) copy-start(f32[3072]{0:T(1024)} %param.20) | copy-start | bytes 36868
  19.2 14.2 %copy-start.3 = (f32[128]{0:T(128)S(1)}, f32[128]{0:T(128)}, u32[]{:S(2)}) copy-start(f32[128]{0:T(128)} %param.23) | copy-start | bytes 1540
  25.1 13.4 %collective-permute-start.3 = (bf16[144,512]{1,0:T(8,128)(2,1)S(1)}, bf16[144,512]{1,0:T(8,128)(2,1)S(1)}, u32[]{:S(2)}, u32[]{:S(2)}) collective-permute-start(bf16[144,512]{1,0:T(8,128)(2,1)S(1)} %get-tuple-element.23.s0), channel_id=1, source_target_pairs={{0,1},{1,2},{2,3},{3,0},{4,5},{5,6},{6,7},{7,4},{8,9},{9,10},{10,1... | collective-permute-start | bytes 442376 | tf_op jit(solution)/shard_map/ppermute | solution.py:107
  26.7 11.8 %collective-permute-start.4 = (bf16[144,512]{1,0:T(8,128)(2,1)S(1)}, bf16[144,512]{1,0:T(8,128)(2,1)S(1)}, u32[]{:S(2)}, u32[]{:S(2)}) collective-permute-start(bf16[144,512]{1,0:T(8,128)(2,1)S(1)} %get-tuple-element.23.s0), channel_id=1, source_target_pairs={{0,3},{1,0},{2,1},{3,2},{4,7},{5,4},{6,5},{7,6},{8,11},{9,8},{10,9... | collective-permute-start | bytes 442376 | tf_op jit(solution)/shard_map/ppermute | solution.py:107
  28.4 10.2 %collective-permute-start.5 = (bf16[144,512]{1,0:T(8,128)(2,1)S(1)}, bf16[144,512]{1,0:T(8,128)(2,1)S(1)}, u32[]{:S(2)}, u32[]{:S(2)}) collective-permute-start(bf16[144,512]{1,0:T(8,128)(2,1)S(1)} %get-tuple-element.23.s0), channel_id=1, source_target_pairs={{0,2},{1,3},{2,0},{3,1},{4,6},{5,7},{6,4},{7,5},{8,10},{9,11},{10,... | collective-permute-start | bytes 442376 | tf_op jit(solution)/shard_map/ppermute | solution.py:107
  30.1 8.5 %collective-permute-start.6 = (bf16[144,512]{1,0:T(8,128)(2,1)S(1)}, bf16[144,512]{1,0:T(8,128)(2,1)S(1)}, u32[]{:S(2)}, u32[]{:S(2)}) collective-permute-start(bf16[144,512]{1,0:T(8,128)(2,1)S(1)} %get-tuple-element.23.s0), channel_id=1, source_target_pairs={{0,64},{4,68},{8,72},{12,76},{16,80},{20,84},{24,88},{28,92},{32,9... | collective-permute-start | bytes 442376 | tf_op jit(solution)/shard_map/ppermute | solution.py:103
  32.2 8.5 %collective-permute-start.7 = (bf16[144,512]{1,0:T(8,128)(2,1)S(1)}, bf16[144,512]{1,0:T(8,128)(2,1)S(1)}, u32[]{:S(2)}, u32[]{:S(2)}) collective-permute-start(bf16[144,512]{1,0:T(8,128)(2,1)S(1)} %get-tuple-element.23.s0), channel_id=1, source_target_pairs={{0,68},{4,64},{8,76},{12,72},{16,84},{20,80},{24,92},{28,88},{32,1... | collective-permute-start | bytes 442376 | tf_op jit(solution)/shard_map/ppermute | solution.py:103
  41.9 11.4 %collective-permute-start.11 = (bf16[288,512]{1,0:T(8,128)(2,1)S(1)}, bf16[288,512]{1,0:T(8,128)(2,1)S(1)}, u32[]{:S(2)}, u32[]{:S(2)}) collective-permute-start(bf16[288,512]{1,0:T(8,128)(2,1)S(1)} %get-tuple-element.29.g0), channel_id=1, source_target_pairs={{0,2},{1,3},{2,0},{3,1},{4,6},{5,7},{6,4},{7,5},{8,10},{9,11},{10,... | collective-permute-start | bytes 884744 | tf_op jit(solution)/shard_map/ppermute | solution.py:107
  43.8 14.4 %collective-permute-start.10 = (bf16[528,512]{1,0:T(8,128)(2,1)S(1)}, bf16[528,512]{1,0:T(8,128)(2,1)S(1)}, u32[]{:S(2)}, u32[]{:S(2)}) collective-permute-start(bf16[528,512]{1,0:T(8,128)(2,1)S(1)} %get-tuple-element.28.a0), channel_id=1, source_target_pairs={{0,32},{4,36},{8,40},{12,44},{16,48},{20,52},{24,56},{28,60},{32,6... | collective-permute-start | bytes 1622024 | tf_op jit(solution)/shard_map/ppermute | solution.py:103
  45.3 15.5 %collective-permute-start.13 = (bf16[528,512]{1,0:T(8,128)(2,1)S(1)}, bf16[528,512]{1,0:T(8,128)(2,1)S(1)}, u32[]{:S(2)}, u32[]{:S(2)}) collective-permute-start(bf16[528,512]{1,0:T(8,128)(2,1)S(1)} %get-tuple-element.28.a0), channel_id=1, source_target_pairs={{0,96},{4,100},{8,104},{12,108},{16,112},{20,116},{24,120},{28,124... | collective-permute-start | bytes 1622024 | tf_op jit(solution)/shard_map/ppermute | solution.py:103
  45.8 12.4 %collective-permute-start.8 = (bf16[3,512,128]{2,1,0:T(8,128)(2,1)S(1)}, bf16[3,512,128]{2,1,0:T(8,128)(2,1)S(1)}, u32[]{:S(2)}, u32[]{:S(2)}) collective-permute-start(bf16[3,512,128]{2,1,0:T(8,128)(2,1)S(1)} %get-tuple-element.27.refs_0_), channel_id=1, source_target_pairs={{0,16},{4,20},{8,24},{12,28},{16,0},{20,4},{24,8},{28,12},{32,48},... | collective-permute-start | bytes 1179656 | tf_op jit(solution)/shard_map/ppermute | solution.py:103
  49.6 9.5 %collective-permute-start.14 = (bf16[288,512]{1,0:T(8,128)(2,1)S(1)}, bf16[288,512]{1,0:T(8,128)(2,1)S(1)}, u32[]{:S(2)}, u32[]{:S(2)}) collective-permute-start(bf16[288,512]{1,0:T(8,128)(2,1)S(1)} %get-tuple-element.29.g0), channel_id=1, source_target_pairs={{0,1},{1,2},{2,3},{3,0},{4,5},{5,6},{6,7},{7,4},{8,9},{9,10},{10,1... | collective-permute-start | bytes 884744 | tf_op jit(solution)/shard_map/ppermute | solution.py:107
  53.3 7.5 %collective-permute-start.15 = (bf16[288,512]{1,0:T(8,128)(2,1)S(1)}, bf16[288,512]{1,0:T(8,128)(2,1)S(1)}, u32[]{:S(2)}, u32[]{:S(2)}) collective-permute-start(bf16[288,512]{1,0:T(8,128)(2,1)S(1)} %get-tuple-element.29.g0), channel_id=1, source_target_pairs={{0,3},{1,0},{2,1},{3,2},{4,7},{5,4},{6,5},{7,6},{8,11},{9,8},{10,9... | collective-permute-start | bytes 884744 | tf_op jit(solution)/shard_map/ppermute | solution.py:107
  58.2 6.0 %collective-permute-start.9 = (bf16[528,512]{1,0:T(8,128)(2,1)S(1)}, bf16[528,512]{1,0:T(8,128)(2,1)S(1)}, u32[]{:S(2)}, u32[]{:S(2)}) collective-permute-start(bf16[528,512]{1,0:T(8,128)(2,1)S(1)} %get-tuple-element.28.a0), channel_id=1, source_target_pairs={{0,4},{4,0},{8,12},{12,8},{16,20},{20,16},{24,28},{28,24},{32,36},... | collective-permute-start | bytes 1622024 | tf_op jit(solution)/shard_map/ppermute | solution.py:103
  58.3 6.0 %collective-permute-start.12 = (bf16[528,512]{1,0:T(8,128)(2,1)S(1)}, bf16[528,512]{1,0:T(8,128)(2,1)S(1)}, u32[]{:S(2)}, u32[]{:S(2)}) collective-permute-start(bf16[528,512]{1,0:T(8,128)(2,1)S(1)} %shard_map.135.a1), channel_id=1, source_target_pairs={{0,4},{4,0},{8,12},{12,8},{16,20},{20,16},{24,28},{28,24},{32,36},... | collective-permute-start | bytes 1622024 | tf_op jit(solution)/shard_map/ppermute | solution.py:103
  60.8 3.4 %collective-permute-start.16 = (bf16[528,512]{1,0:T(8,128)(2,1)S(1)}, bf16[528,512]{1,0:T(8,128)(2,1)S(1)}, u32[]{:S(2)}, u32[]{:S(2)}) collective-permute-start(bf16[528,512]{1,0:T(8,128)(2,1)S(1)} %shard_map.136.a3), channel_id=1, source_target_pairs={{0,4},{4,0},{8,12},{12,8},{16,20},{20,16},{24,28},{28,24},{32,36},... | collective-permute-start | bytes 1622024 | tf_op jit(solution)/shard_map/ppermute | solution.py:103
  60.9 20.2 %collective-permute-start.18 = (bf16[3,512,128]{2,1,0:T(8,128)(2,1)S(1)}, bf16[3,512,128]{2,1,0:T(8,128)(2,1)S(1)}, u32[]{:S(2)}, u32[]{:S(2)}) collective-permute-start(bf16[3,512,128]{2,1,0:T(8,128)(2,1)S(1)} %get-tuple-element.27.refs_0_), channel_id=1, source_target_pairs={{0,8},{4,12},{8,16},{12,20},{16,24},{20,28},{24,0},{28,4},{32,40},... | collective-permute-start | bytes 1179656 | tf_op jit(solution)/shard_map/ppermute | solution.py:103
  62.5 18.7 %collective-permute-start.19 = (bf16[3,512,128]{2,1,0:T(8,128)(2,1)S(1)}, bf16[3,512,128]{2,1,0:T(8,128)(2,1)S(1)}, u32[]{:S(2)}, u32[]{:S(2)}) collective-permute-start(bf16[3,512,128]{2,1,0:T(8,128)(2,1)S(1)} %get-tuple-element.27.refs_0_), channel_id=1, source_target_pairs={{0,24},{4,28},{8,0},{12,4},{16,8},{20,12},{24,16},{28,20},{32,56},... | collective-permute-start | bytes 1179656 | tf_op jit(solution)/shard_map/ppermute | solution.py:103
  78.3 19.7 %collective-permute-start.17 = (bf16[1664,128]{1,0:T(8,128)(2,1)S(1)}, bf16[1664,128]{1,0:T(8,128)(2,1)S(1)}, u32[]{:S(2)}, u32[]{:S(2)}) collective-permute-start(bf16[1664,128]{1,0:T(8,128)(2,1)S(1)} %get-tuple-element.35), channel_id=1, source_target_pairs={{0,16},{4,20},{8,24},{12,28},{16,0},{20,4},{24,8},{28,12},{32,48},... | collective-permute-start | bytes 1277960 | tf_op jit(solution)/shard_map/ppermute | solution.py:103
  95.9 11.4 %collective-permute-start.20 = (bf16[1664,128]{1,0:T(8,128)(2,1)S(1)}, bf16[1664,128]{1,0:T(8,128)(2,1)S(1)}, u32[]{:S(2)}, u32[]{:S(2)}) collective-permute-start(bf16[1664,128]{1,0:T(8,128)(2,1)S(1)} %get-tuple-element.36), channel_id=1, source_target_pairs={{0,24},{4,28},{8,0},{12,4},{16,8},{20,12},{24,16},{28,20},{32,56},... | collective-permute-start | bytes 1277960 | tf_op jit(solution)/shard_map/ppermute | solution.py:103
  96.6 12.5 %collective-permute-start.21 = (bf16[1664,128]{1,0:T(8,128)(2,1)S(1)}, bf16[1664,128]{1,0:T(8,128)(2,1)S(1)}, u32[]{:S(2)}, u32[]{:S(2)}) collective-permute-start(bf16[1664,128]{1,0:T(8,128)(2,1)S(1)} %get-tuple-element.37), channel_id=1, source_target_pairs={{0,8},{4,12},{8,16},{12,20},{16,24},{20,28},{24,0},{28,4},{32,40},... | collective-permute-start | bytes 1277960 | tf_op jit(solution)/shard_map/ppermute | solution.py:103

commit v2 on v1

--- a/solution.py
+++ b/solution.py
@@ -361,11 +361,9 @@
 
 
 def query_kernel(
-    band_ref, s0, s1, s3, s2, x_near, x_far, weight_ref, rows_ref, gain_ref, q_ref, xr_ref, pair_ref
+    band_ref, s0, s1, s3, s2, weight_ref, rows_ref, gain_ref, needed, q_ref, xr_ref
 ):
     shards = (s0, s1, s3, s2)
-    pair_ref[0 : SHARD + 16, :] = x_near[...]
-    pair_ref[SHARD + 16 : 2 * (SHARD + 16), :] = x_far[...]
     sources, across = gather_rows(shards, 0, band_ref[5], xr_ref)
     for ref, source, extra in zip(shards, sources, across):
         scale = jnp.transpose(jnp.broadcast_to(extra[:, 0:HD] + extra[:, HD : 2 * HD], (HD, HD)))
@@ -381,21 +379,33 @@
                 q_ref[head, rows, :] = values[i * 64 : (i + 1) * 64]
 
 
-def queries_of(info, shards, across, weight, rows, gain):
+def queries_of(info, shards, weight, rows, gain, needed):
     return pl.pallas_call(
         query_kernel,
-        in_specs=[SMEM] + [VMEM] * 9,
-        out_specs=[VMEM] * 3,
+        in_specs=[SMEM] + [VMEM] * 7 + [ANY],
+        out_specs=[VMEM] * 2,
         out_shape=[
             jax.ShapeDtypeStruct((HEADS, OWN, HD), BF16),
             jax.ShapeDtypeStruct((OWN + 16, 512), BF16),
-            jax.ShapeDtypeStruct((2 * (SHARD + 16), 512), BF16),
         ],
         compiler_params=params(8),
         cost_estimate=pl.CostEstimate(
             flops=2 * 512 * 512 * 384, bytes_accessed=2000000, transcendentals=0
         ),
-    )(info, *in_vmem(*shards, *across, weight, rows), gain[None] * FACTOR)
+    )(info, *in_vmem(*shards, weight, rows), gain[None] * FACTOR, needed)
+
+
+def assemble(info, shards):
+    def kernel(info_ref, s0, s1, s3, s2, out_ref):
+        gather_rows((s0, s1, s3, s2), 0, info_ref[5], out_ref)
+
+    return pl.pallas_call(
+        kernel,
+        in_specs=[SMEM] + [VMEM] * 4,
+        out_specs=VMEM,
+        out_shape=jax.ShapeDtypeStruct((OWN + 16, 512), BF16),
+        compiler_params=params(4),
+    )(info, *in_vmem(*shards))
 
 
 def store_rows(o_ref, base, results):
@@ -516,38 +526,29 @@
 
 
 def first_kernel(
-    info_ref, q_hbm, a0, b0, a1, b1, a3, b3, g0, g1, g3, g2, wk_hbm, wv_hbm, rows_hbm, cols_hbm,
-    o2, key_out, value_out, key_t, value, blocks, pairs, q2, wk_ref, wv_ref, rows_ref, cols_ref,
+    info_ref, q_hbm, a0, b0, a1, b1, a3, b3, a2, b2, wk_hbm, wv_hbm, rows_hbm, cols_hbm,
+    o2, key_out, value_out, key_t, value, blocks, q2, wk_ref, wv_ref, rows_ref, cols_ref,
     sems,
 ):
     x_here, _, core = place_of(info_ref)
     weight_copies = fetch(
         (wk_hbm, wv_hbm, rows_hbm, cols_hbm), (wk_ref, wv_ref, rows_ref, cols_ref), sems
     )
-    block_copies = fetch((a0, b0, a1, b1, a3, b3), [blocks.at[i] for i in range(6)], sems, 4)
-    pair_copies = fetch((g0, g1, g3, g2), [pairs.at[i] for i in range(4)], sems, 10)
-    (query_copy,) = fetch([q_hbm], [q2], sems, 14)
+    block_copies = fetch(
+        (a0, b0, a1, b1, a3, b3, a2, b2), [blocks.at[i] for i in range(8)], sems, 4
+    )
+    (query_copy,) = fetch([q_hbm], [q2], sems, 12)
     for copy in weight_copies:
         copy.wait()
     for at in range(8):
-        if at == 0:
-            for copy in block_copies:
+        if at % 4 == 0:
+            for copy in block_copies[at : at + 4]:
                 copy.wait()
-        if at == 4:
-            for copy in pair_copies:
-                copy.wait()
-            for swap in range(2):
-                gather_rows(
-                    [pairs.at[i] for i in range(4)],
-                    swap * (SHARD + 16),
-                    info_ref[5],
-                    blocks.at[6 + swap],
-                )
         source = lax.rem(x_here + (NX - (0, 1, 3, 2)[at // 2]), NX)
         core_at = core if at % 2 == 0 else 1 - core
         start = pl.multiple_of((source * 2 + core_at) * OWN, OWN)
         project_block(blocks.at[at], start, wk_ref, wv_ref, rows_ref, cols_ref, key_t, value)
-    copies = fetch((key_t, value), (key_out, value_out), sems, 15)
+    copies = fetch((key_t, value), (key_out, value_out), sems, 13)
     query_copy.wait()
     attend_group(info_ref, 2, q2, o2, key_t, value)
     for copy in copies:
@@ -557,10 +558,10 @@
 PARTIAL = jax.ShapeDtypeStruct((HEADS * OWN + 128, HD), BF16)
 
 
-def attend_first(info, query, near, far, pairs, wk, wv, rows, cols):
+def attend_first(info, query, near, far, wk, wv, rows, cols):
     return pl.pallas_call(
         first_kernel,
-        in_specs=[SMEM] + [ANY] * 15,
+        in_specs=[SMEM] + [ANY] * 13,
         out_specs=[VMEM, ANY, ANY],
         out_shape=[
             PARTIAL,
@@ -571,13 +572,12 @@
             pltpu.VMEM((HEADS, HD, KEYS), BF16),
             pltpu.VMEM((HEADS, KEYS, HD), BF16),
             pltpu.VMEM((8, OWN + 16, 512), BF16),
-            pltpu.VMEM((4, 2 * (SHARD + 16), 512), BF16),
             pltpu.VMEM((HEADS, OWN, HD), BF16),
             pltpu.VMEM((384, 512), BF16),
             pltpu.VMEM((512, 384), BF16),
             pltpu.VMEM((8, 1152), F32),
             pltpu.VMEM((3, 384, HD), F32),
-            pltpu.SemaphoreType.DMA((17,)),
+            pltpu.SemaphoreType.DMA((15,)),
         ],
         compiler_params=params(34),
         cost_estimate=pl.CostEstimate(
@@ -587,7 +587,6 @@
         info,
         query,
         *[block for pair in zip(near, far) for block in pair],
-        *pairs,
         wk,
         wv,
         rows,
@@ -700,16 +699,17 @@
         embed_near, embed_bias, mod_shift, mod_scale, k_gain, qkv_near
     )
     shards = (send, shift_band(send, 1), shift_band(send, 3), shift_band(send, 2))
-    across = (shift_tm(send, dx=2), shift_tm(send, dx=2, swap=True))
-    query, xr, pair = queries_of(info, shards, across, wq, rows, q_gain)
+    across = shift_tm(send, dx=2)
+    query, xr = queries_of(info, shards, wq, rows, q_gain, across)
     far_own = shift_tm(xr, swap=True)
     q1, q3, q2 = shift_tm(query, dz=1), shift_tm(query, dz=3), shift_tm(query, dz=2)
-    pairs = (pair, shift_band(pair, 1), shift_band(pair, 3), shift_band(pair, 2))
-    a1 = after(shift_tm(xr, dx=1), q2, pairs[3])
-    a3 = after(shift_tm(xr, dx=3), pairs[1], pairs[2])
-    near = (xr, a1, a3)
-    far = (far_own, shift_tm(a1, swap=True), shift_tm(a3, swap=True))
-    o2, key_t, value = attend_first(info, q2, near, far, pairs, wk, wv, rows, cols)
+    g1, g3, g2 = shift_band(across, 1), shift_band(across, 3), shift_band(across, 2)
+    a1 = after(shift_tm(xr, dx=1), q2, g2)
+    a3 = after(shift_tm(xr, dx=3), g1, g3)
+    a2 = assemble(info, (across, g1, g3, g2))
+    near = (xr, a1, a3, a2)
+    far = (far_own,) + tuple(shift_tm(part, swap=True) for part in near[1:])
+    o2, key_t, value = attend_first(info, q2, near, far, wk, wv, rows, cols)
     p2 = shift_tm(o2, dz=2)
     o1, o3 = attend_next((1, 3), info, (q1, q3), key_t, value)
     p1, p3 = shift_tm(o1, dz=3), shift_tm(o3, dz=1)

time: 111 us -> 110 us (level); the launches traced: 111 us -> 108 us
  starting transfers between devices: 32.7 us -> 28.3 us
    ppermute x6, waiting for transfers between devices: 5.19 us -> 11 us  [shift_band(): return lax.ppermute(block, 'band', [(i, (i + db) % NB) for i in range(NB)])]
    ppermute x13, waiting for transfers between devices: 9.95 us -> 4.86 us  [shift_tm(): return lax.ppermute(block, 'tm', route)]
    ppermute x13, starting transfers between devices: 18.2 us -> 14.4 us  [shift_tm(): return lax.ppermute(block, 'tm', route)]
    pallas_call x2 -> x3, Pallas kernels: 15.2 us -> 15.6 us  [the longest x1 13.8 us: attend_first(): pl.pallas_call(first_kernel, in_specs=[SMEM] + [ANY] * 13, out_specs=[VME...]
  transfers between devices with their start and end apart: 22 -> 22, of which waited for: 9 -> 8; matrix products, arithmetic and copies ran while one was open for 2% -> 2% of each run, Pallas kernels for 42% -> 44%
where the time goes in v2:
time: 110 us; the launch traced here: 108 us
  Pallas kernels  56.3 us (51%)
  starting transfers between devices  28.3 us (26%)
  waiting for transfers between devices  19.3 us (18%)
  local copies, waits for them, and re-layouts  1.67 us (2%)
  other arithmetic  1.39 us (1%)
    pallas_call x2, Pallas kernels, attend_next(): pl.pallas_call(functools.partial(next_kernel, groups), in_specs=[SMEM, VM...  22.4 us
    ppermute x13, starting transfers between devices, shift_tm(): return lax.ppermute(block, 'tm', route)  14.4 us
    pallas_call x1, Pallas kernels, attend_first(): pl.pallas_call(first_kernel, in_specs=[SMEM] + [ANY] * 13, out_specs=[VME...  13.8 us
    ppermute x6, waiting for transfers between devices, shift_band(): return lax.ppermute(block, 'band', [(i, (i + db) % NB) for i in range(NB)])  11 us
    ppermute x6, starting transfers between devices, shift_band(): return lax.ppermute(block, 'band', [(i, (i + db) % NB) for i in range(NB)])  7.2 us
    ppermute x3, starting transfers between devices, halo(): return lax.ppermute(block, ('tm', 'band'), route)  6.67 us
    pallas_call x1, Pallas kernels, conv(): pl.pallas_call(conv_kernel, in_specs=[SMEM] + [VMEM] * 4 + [HBM] * 4, out...  5.82 us
    pallas_call x1, Pallas kernels, conv_newest(): pl.pallas_call(newest_kernel, in_specs=[VMEM] + [HBM] * 4, out_specs=[VME...  5.4 us
  transfers between devices with their start and end apart: 22, of which 8 were waited for; matrix products, arithmetic and copies ran while one was open for 2% of the time, Pallas kernels for 44%

profile of v2, /device:TPU:2, one launch (start us, length us, event | category | flops | bytes accessed | tf_op | source)
XLA Modules:
  0.0 107.7 jit_solution(4263161679654898675)
XLA Ops:
  0.6 0.7 fusion
  1.4 3.5 %collective-permute-start = (bf16[2,1,8,512]{3,2,1,0:T(8,128)(2,1)S(1)}, bf16[2,1,8,512]{3,2,1,0:T(8,128)(2,1)S(1)}, u32[]{:S(2)}, u32[]{:S(2)}) collective-permute-start(bf16[2,1,8,512]{3,2,1,0:T(8,128)(2,1)S(1)} %get-tuple-element.37), channel_id=1, source_target_pairs={{0,1},{1,2},{2,3},{4,5},{5,6},{6,7},{8,9},{9,10},{10,11},{12,13},{... | collective-permute-start | bytes 49160 | tf_op jit(solution)/shard_map/ppermute | solution.py:117
  4.8 1.3 %collective-permute-start.1 = (bf16[2,1,8,512]{3,2,1,0:T(8,128)(2,1)S(1)}, bf16[2,1,8,512]{3,2,1,0:T(8,128)(2,1)S(1)}, u32[]{:S(2)}, u32[]{:S(2)}) collective-permute-start(bf16[2,1,8,512]{3,2,1,0:T(8,128)(2,1)S(1)} %get-tuple-element.36), channel_id=1, source_target_pairs={{1,0},{2,1},{3,2},{5,4},{6,5},{7,6},{9,8},{10,9},{11,10},{13,12},{... | collective-permute-start | bytes 49160 | tf_op jit(solution)/shard_map/ppermute | solution.py:117
  6.1 0.7 multiply_bitcast_fusion.gain_ref
  6.8 0.9 constant_dynamic-update-slice_fusion.1
  7.7 2.7 %collective-permute-done.1 = bf16[2,1,8,512]{3,2,1,0:T(8,128)(2,1)S(1)} collective-permute-done((bf16[2,1,8,512]{3,2,1,0:T(8,128)(2,1)S(1)}, bf16[2,1,8,512]{3,2,1,0:T(8,128)(2,1)S(1)}, u32[]{:S(2)}, u32[]{:S(2)}) %collective-permute-start.1) | collective-permute-done | bytes 16416 | tf_op jit(solution)/shard_map/ppermute | solution.py:117
  10.5 1.9 %collective-permute-start.2 = (bf16[2,10,8,512]{3,2,1,0:T(8,128)(2,1)S(1)}, bf16[2,10,8,512]{3,2,1,0:T(8,128)(2,1)S(1)}, u32[]{:S(2)}, u32[]{:S(2)}) collective-permute-start(bf16[2,10,8,512]{3,2,1,0:T(8,128)(2,1)S(1)} %constant_dynamic-update-slice_fusion.cur_ref), channel_id=1, source_target_pairs={{0,4},{1,5},{2,6},{3,7},{4,8},{5,9},{6,10},{7,11},{8,12},{9,13},{1... | collective-permute-start | bytes 491528 | tf_op jit(solution)/shard_map/ppermute | solution.py:117
  12.4 0.7 pad_add_fusion.info_ref.band_ref
  13.1 5.4 %shard_map.131 = (f32[128,512]{1,0:T(8,128)S(1)}, bf16[512,3072]{1,0:T(8,128)(2,1)S(1)}, bf16[9,3072,128]{2,1,0:T(8,128)(2,1)S(1)}) custom-call(bf16[2,10,8,512]{3,2,1,0:T(8,128)(2,1)S(1)} %constant_dynamic-update-slice_fusion.cur_ref, f32[1,512]{1,0:T(1,128)} %bitcast.21, bf16[3,3,3,512,512]{4,3,2,1,0:T(8,128)(2,1)} %weight_hbm.3, ...), custom_call_target="tpu_custom_call" | custom-call | flops 603979776 | bytes 15000000 | tf_op jit(solution)/shard_map/pallas_call | solution.py:225
  18.5 0.7 collective-permute-done.2.prev_ref
  19.2 5.8 %shard_map.132 = (bf16[2,8,8,512]{3,2,1,0:T(8,128)(2,1)}, bf16[144,512]{1,0:T(8,128)(2,1)S(1)}) custom-call(s32[6]{0:T(128)S(1)} %pad_add_fusion.info_ref.band_ref, bf16[2,10,8,512]{3,2,1,0:T(8,128)(2,1)S(1)} %constant_dynamic-update-slice_fusion.cur_ref, bf16[2,10,8,512]{3,2,1,0:T(8,128)(2,1)S(1)} %collective-permute-done.2.prev_ref, ...), custom_call_target="tpu_custom_call" | custom-call | flops 1811939328 | bytes 12000000 | tf_op jit(solution)/shard_map/pallas_call | solution.py:304
  25.1 1.6 %collective-permute-start.3 = (bf16[144,512]{1,0:T(8,128)(2,1)S(1)}, bf16[144,512]{1,0:T(8,128)(2,1)S(1)}, u32[]{:S(2)}, u32[]{:S(2)}) collective-permute-start(bf16[144,512]{1,0:T(8,128)(2,1)S(1)} %get-tuple-element.22.s0), channel_id=1, source_target_pairs={{0,1},{1,2},{2,3},{3,0},{4,5},{5,6},{6,7},{7,4},{8,9},{9,10},{10,1... | collective-permute-start | bytes 442376 | tf_op jit(solution)/shard_map/ppermute | solution.py:107
  26.7 1.7 %collective-permute-start.4 = (bf16[144,512]{1,0:T(8,128)(2,1)S(1)}, bf16[144,512]{1,0:T(8,128)(2,1)S(1)}, u32[]{:S(2)}, u32[]{:S(2)}) collective-permute-start(bf16[144,512]{1,0:T(8,128)(2,1)S(1)} %get-tuple-element.22.s0), channel_id=1, source_target_pairs={{0,3},{1,0},{2,1},{3,2},{4,7},{5,4},{6,5},{7,6},{8,11},{9,8},{10,9... | collective-permute-start | bytes 442376 | tf_op jit(solution)/shard_map/ppermute | solution.py:107
  28.4 1.7 %collective-permute-start.5 = (bf16[144,512]{1,0:T(8,128)(2,1)S(1)}, bf16[144,512]{1,0:T(8,128)(2,1)S(1)}, u32[]{:S(2)}, u32[]{:S(2)}) collective-permute-start(bf16[144,512]{1,0:T(8,128)(2,1)S(1)} %get-tuple-element.22.s0), channel_id=1, source_target_pairs={{0,2},{1,3},{2,0},{3,1},{4,6},{5,7},{6,4},{7,5},{8,10},{9,11},{10,... | collective-permute-start | bytes 442376 | tf_op jit(solution)/shard_map/ppermute | solution.py:107
  30.1 2.1 %collective-permute-start.6 = (bf16[144,512]{1,0:T(8,128)(2,1)S(1)}, bf16[144,512]{1,0:T(8,128)(2,1)S(1)}, u32[]{:S(2)}, u32[]{:S(2)}) collective-permute-start(bf16[144,512]{1,0:T(8,128)(2,1)S(1)} %get-tuple-element.22.s0), channel_id=1, source_target_pairs={{0,64},{4,68},{8,72},{12,76},{16,80},{20,84},{24,88},{28,92},{32,9... | collective-permute-start | bytes 442376 | tf_op jit(solution)/shard_map/ppermute | solution.py:103
  32.2 5.0 %shard_map.133 = (bf16[512,384]{1,0:T(8,128)(2,1)S(1)}, bf16[384,512]{1,0:T(8,128)(2,1)S(1)}, bf16[512,384]{1,0:T(8,128)(2,1)S(1)}, f32[8,1152]{1,0:T(8,128)S(1)}, f32[3,384,128]{2,1,0:T(8,128)S(1)}) custom-call(bf16[512,3072]{1,0:T(8,128)(2,1)S(1)} %get-tuple-element.20.embed_ref, f32[1,3072]{1,0:T(1,128)S(1)} %bitcast.15, f32[1,3072]{1,0:T(1,128)S(1)} %bitcast.16, ...), custom_call_target="tpu_custom_call" | custom-call | flops 3737124864 | bytes 12000000 | tf_op jit(solution)/shard_map/pallas_call | solution.py:161
  37.9 1.2 %shard_map.134 = (bf16[3,512,128]{2,1,0:T(8,128)(2,1)S(1)}, bf16[528,512]{1,0:T(8,128)(2,1)S(1)}) custom-call(s32[6]{0:T(128)S(1)} %pad_add_fusion.info_ref.band_ref, bf16[144,512]{1,0:T(8,128)(2,1)S(1)} %get-tuple-element.22.s0, bf16[144,512]{1,0:T(8,128)(2,1)S(1)} %collective-permute-done.3.s1, bf16[144,512]{1,0:T(8,128)(2,1)S(1)} %collective-permute-done.4.s3, ...), custom_call_target="tpu_custom_call" | custom-call | flops 201326592 | bytes 2000000 | tf_op jit(solution)/shard_map/pallas_call | solution.py:383
  39.0 1.6 %collective-permute-start.9 = (bf16[528,512]{1,0:T(8,128)(2,1)S(1)}, bf16[528,512]{1,0:T(8,128)(2,1)S(1)}, u32[]{:S(2)}, u32[]{:S(2)}) collective-permute-start(bf16[528,512]{1,0:T(8,128)(2,1)S(1)} %get-tuple-element.27.a0), channel_id=1, source_target_pairs={{0,32},{4,36},{8,40},{12,44},{16,48},{20,52},{24,56},{28,60},{32,6... | collective-permute-start | bytes 1622024 | tf_op jit(solution)/shard_map/ppermute | solution.py:103
  41.1 3.6 %collective-permute-start.7 = (bf16[3,512,128]{2,1,0:T(8,128)(2,1)S(1)}, bf16[3,512,128]{2,1,0:T(8,128)(2,1)S(1)}, u32[]{:S(2)}, u32[]{:S(2)}) collective-permute-start(bf16[3,512,128]{2,1,0:T(8,128)(2,1)S(1)} %get-tuple-element.26.refs_0_), channel_id=1, source_target_pairs={{0,16},{4,20},{8,24},{12,28},{16,0},{20,4},{24,8},{28,12},{32,48},... | collective-permute-start | bytes 1179656 | tf_op jit(solution)/shard_map/ppermute | solution.py:103
  44.7 1.8 %collective-permute-start.10 = (bf16[144,512]{1,0:T(8,128)(2,1)S(1)}, bf16[144,512]{1,0:T(8,128)(2,1)S(1)}, u32[]{:S(2)}, u32[]{:S(2)}) collective-permute-start(bf16[144,512]{1,0:T(8,128)(2,1)S(1)} %collective-permute-done.6.needed.s0), channel_id=1, source_target_pairs={{0,2},{1,3},{2,0},{3,1},{4,6},{5,7},{6,4},{7,5},{8,10},{9,11},{10,... | collective-permute-start | bytes 442376 | tf_op jit(solution)/shard_map/ppermute | solution.py:107
  46.9 5.8 %collective-permute-done.10.refs_1_.s2 = bf16[144,512]{1,0:T(8,128)(2,1)S(1)} collective-permute-done((bf16[144,512]{1,0:T(8,128)(2,1)S(1)}, bf16[144,512]{1,0:T(8,128)(2,1)S(1)}, u32[]{:S(2)}, u32[]{:S(2)}) %collective-permute-start.10) | collective-permute-done | bytes 147488 | tf_op jit(solution)/shard_map/ppermute | solution.py:107
  52.8 1.5 %collective-permute-done.13.refs_0_.s1 = bf16[144,512]{1,0:T(8,128)(2,1)S(1)} collective-permute-done((bf16[144,512]{1,0:T(8,128)(2,1)S(1)}, bf16[144,512]{1,0:T(8,128)(2,1)S(1)}, u32[]{:S(2)}, u32[]{:S(2)}) %collective-permute-start.13) | collective-permute-done | bytes 147488 | tf_op jit(solution)/shard_map/ppermute | solution.py:107
  54.3 3.6 %collective-permute-done.14.refs_1_.s3 = bf16[144,512]{1,0:T(8,128)(2,1)S(1)} collective-permute-done((bf16[144,512]{1,0:T(8,128)(2,1)S(1)}, bf16[144,512]{1,0:T(8,128)(2,1)S(1)}, u32[]{:S(2)}, u32[]{:S(2)}) %collective-permute-start.14) | collective-permute-done | bytes 147488 | tf_op jit(solution)/shard_map/ppermute | solution.py:107
  57.9 0.7 shard_map.137.a2
  59.7 3.2 %collective-permute-start.19 = (bf16[3,512,128]{2,1,0:T(8,128)(2,1)S(1)}, bf16[3,512,128]{2,1,0:T(8,128)(2,1)S(1)}, u32[]{:S(2)}, u32[]{:S(2)}) collective-permute-start(bf16[3,512,128]{2,1,0:T(8,128)(2,1)S(1)} %get-tuple-element.26.refs_0_), channel_id=1, source_target_pairs={{0,24},{4,28},{8,0},{12,4},{16,8},{20,12},{24,16},{28,20},{32,56},... | collective-permute-start | bytes 1179656 | tf_op jit(solution)/shard_map/ppermute | solution.py:103
  63.0 13.8 %shard_map.138 = (bf16[1664,128]{1,0:T(8,128)(2,1)S(1)}, bf16[3,128,4096]{2,1,0:T(8,128)(2,1)S(1)}, bf16[3,4096,128]{2,1,0:T(8,128)(2,1)S(1)}) custom-call(s32[6]{0:T(128)S(1)} %pad_add_fusion.info_ref.band_ref, bf16[3,512,128]{2,1,0:T(8,128)(2,1)S(1)} %collective-permute-done.7.refs_0_.q_hbm, bf16[528,512]{1,0:T(8,128)(2,1)S(1)} %get-tuple-element.27.a0, ...), custom_call_target="tpu_custom_call" | custom-call | flops 15000000512 | bytes 10000000 | tf_op jit(solution)/shard_map/pallas_call | solution.py:562
  77.1 14.7 %shard_map.140 = (bf16[1664,128]{1,0:T(8,128)(2,1)S(1)}, bf16[1664,128]{1,0:T(8,128)(2,1)S(1)}) custom-call(s32[6]{0:T(128)S(1)} %pad_add_fusion.info_ref.band_ref, bf16[3,128,4096]{2,1,0:T(8,128)(2,1)S(1)} %get-tuple-element.31.key_t, bf16[3,4096,128]{2,1,0:T(8,128)(2,1)S(1)} %get-tuple-element.32.value, ...), custom_call_target="tpu_custom_call" | custom-call | flops 16000000000 | bytes 8000000 | tf_op jit(solution)/shard_map/pallas_call | solution.py:618
  91.8 1.5 %collective-permute-start.20 = (bf16[1664,128]{1,0:T(8,128)(2,1)S(1)}, bf16[1664,128]{1,0:T(8,128)(2,1)S(1)}, u32[]{:S(2)}, u32[]{:S(2)}) collective-permute-start(bf16[1664,128]{1,0:T(8,128)(2,1)S(1)} %get-tuple-element.34), channel_id=1, source_target_pairs={{0,24},{4,28},{8,0},{12,4},{16,8},{20,12},{24,16},{28,20},{32,56},... | collective-permute-start | bytes 1277960 | tf_op jit(solution)/shard_map/ppermute | solution.py:103
  93.9 7.6 %shard_map.139.p0 = bf16[1664,128]{1,0:T(8,128)(2,1)S(1)} custom-call(s32[6]{0:T(128)S(1)} %pad_add_fusion.info_ref.band_ref, bf16[3,128,4096]{2,1,0:T(8,128)(2,1)S(1)} %get-tuple-element.31.key_t, bf16[3,4096,128]{2,1,0:T(8,128)(2,1)S(1)} %get-tuple-element.32.value, bf16[3,512,128]{2,1,0:T(8,128)(2,1)S(1)} %get-tuple-element.26.refs_0_, ...), custom_call_target="tpu_custom_call" | custom-call | flops 8000000000 | bytes 8000000 | tf_op jit(solution)/shard_map/pallas_call | solution.py:618
  101.5 1.9 %collective-permute-done.20.p1 = bf16[1664,128]{1,0:T(8,128)(2,1)S(1)} collective-permute-done((bf16[1664,128]{1,0:T(8,128)(2,1)S(1)}, bf16[1664,128]{1,0:T(8,128)(2,1)S(1)}, u32[]{:S(2)}, u32[]{:S(2)}) %collective-permute-start.20) | collective-permute-done | bytes 426016 | tf_op jit(solution)/shard_map/ppermute | solution.py:103
  103.5 2.3 %collective-permute-done.21.p2 = bf16[1664,128]{1,0:T(8,128)(2,1)S(1)} collective-permute-done((bf16[1664,128]{1,0:T(8,128)(2,1)S(1)}, bf16[1664,128]{1,0:T(8,128)(2,1)S(1)}, u32[]{:S(2)}, u32[]{:S(2)}) %collective-permute-start.21) | collective-permute-done | bytes 426016 | tf_op jit(solution)/shard_map/ppermute | solution.py:103
  105.8 1.9 %shard_map.141 = bf16[3,512,128]{2,1,0:T(8,128)(2,1)} custom-call(bf16[1664,128]{1,0:T(8,128)(2,1)S(1)} %shard_map.139.p0, bf16[1664,128]{1,0:T(8,128)(2,1)S(1)} %collective-permute-done.20.p1, bf16[1664,128]{1,0:T(8,128)(2,1)S(1)} %collective-permute-done.21.p2, bf16[1664,128]{1,0:T(8,128)(2,1)S(1)} %collective-permute-done.17.refs_1_.p3), custom_call_target="tpu_custom_call" | custom-call | tf_op jit(solution)/shard_map/pallas_call | solution.py:663
  (37 shorter events, 3.5 us)
Async XLA Ops:
  1.4 5.4 %collective-permute-start = (bf16[2,1,8,512]{3,2,1,0:T(8,128)(2,1)S(1)}, bf16[2,1,8,512]{3,2,1,0:T(8,128)(2,1)S(1)}, u32[]{:S(2)}, u32[]{:S(2)}) collective-permute-start(bf16[2,1,8,512]{3,2,1,0:T(8,128)(2,1)S(1)} %get-tuple-element.37), channel_id=1, source_target_pairs={{0,1},{1,2},{2,3},{4,5},{5,6},{6,7},{8,9},{9,10},{10,11},{12,13},{... | collective-permute-start | bytes 49160 | tf_op jit(solution)/shard_map/ppermute | solution.py:117
  4.8 5.6 %collective-permute-start.1 = (bf16[2,1,8,512]{3,2,1,0:T(8,128)(2,1)S(1)}, bf16[2,1,8,512]{3,2,1,0:T(8,128)(2,1)S(1)}, u32[]{:S(2)}, u32[]{:S(2)}) collective-permute-start(bf16[2,1,8,512]{3,2,1,0:T(8,128)(2,1)S(1)} %get-tuple-element.36), channel_id=1, source_target_pairs={{1,0},{2,1},{3,2},{5,4},{6,5},{7,6},{9,8},{10,9},{11,10},{13,12},{... | collective-permute-start | bytes 49160 | tf_op jit(solution)/shard_map/ppermute | solution.py:117
  10.5 8.7 %collective-permute-start.2 = (bf16[2,10,8,512]{3,2,1,0:T(8,128)(2,1)S(1)}, bf16[2,10,8,512]{3,2,1,0:T(8,128)(2,1)S(1)}, u32[]{:S(2)}, u32[]{:S(2)}) collective-permute-start(bf16[2,10,8,512]{3,2,1,0:T(8,128)(2,1)S(1)} %constant_dynamic-update-slice_fusion.cur_ref), channel_id=1, source_target_pairs={{0,4},{1,5},{2,6},{3,7},{4,8},{5,9},{6,10},{7,11},{8,12},{9,13},{1... | collective-permute-start | bytes 491528 | tf_op jit(solution)/shard_map/ppermute | solution.py:117
  19.2 13.0 %copy-start = (f32[3072]{0:T(1024)S(1)}, f32[3072]{0:T(1024)}, u32[]{:S(2)}) copy-start(f32[3072]{0:T(1024)} %param.18) | copy-start | bytes 36868
  19.2 13.0 %copy-start.1 = (f32[3072]{0:T(1024)S(1)}, f32[3072]{0:T(1024)}, u32[]{:S(2)}) copy-start(f32[3072]{0:T(1024)} %param.19) | copy-start | bytes 36868
  19.2 13.0 %copy-start.2 = (f32[3072]{0:T(1024)S(1)}, f32[3072]{0:T(1024)}, u32[]{:S(2)}) copy-start(f32[3072]{0:T(1024)} %param.20) | copy-start | bytes 36868
  19.2 13.0 %copy-start.3 = (f32[128]{0:T(128)S(1)}, f32[128]{0:T(128)}, u32[]{:S(2)}) copy-start(f32[128]{0:T(128)} %param.23) | copy-start | bytes 1540
  25.1 12.2 %collective-permute-start.3 = (bf16[144,512]{1,0:T(8,128)(2,1)S(1)}, bf16[144,512]{1,0:T(8,128)(2,1)S(1)}, u32[]{:S(2)}, u32[]{:S(2)}) collective-permute-start(bf16[144,512]{1,0:T(8,128)(2,1)S(1)} %get-tuple-element.22.s0), channel_id=1, source_target_pairs={{0,1},{1,2},{2,3},{3,0},{4,5},{5,6},{6,7},{7,4},{8,9},{9,10},{10,1... | collective-permute-start | bytes 442376 | tf_op jit(solution)/shard_map/ppermute | solution.py:107
  26.7 10.5 %collective-permute-start.4 = (bf16[144,512]{1,0:T(8,128)(2,1)S(1)}, bf16[144,512]{1,0:T(8,128)(2,1)S(1)}, u32[]{:S(2)}, u32[]{:S(2)}) collective-permute-start(bf16[144,512]{1,0:T(8,128)(2,1)S(1)} %get-tuple-element.22.s0), channel_id=1, source_target_pairs={{0,3},{1,0},{2,1},{3,2},{4,7},{5,4},{6,5},{7,6},{8,11},{9,8},{10,9... | collective-permute-start | bytes 442376 | tf_op jit(solution)/shard_map/ppermute | solution.py:107
  28.4 8.9 %collective-permute-start.5 = (bf16[144,512]{1,0:T(8,128)(2,1)S(1)}, bf16[144,512]{1,0:T(8,128)(2,1)S(1)}, u32[]{:S(2)}, u32[]{:S(2)}) collective-permute-start(bf16[144,512]{1,0:T(8,128)(2,1)S(1)} %get-tuple-element.22.s0), channel_id=1, source_target_pairs={{0,2},{1,3},{2,0},{3,1},{4,6},{5,7},{6,4},{7,5},{8,10},{9,11},{10,... | collective-permute-start | bytes 442376 | tf_op jit(solution)/shard_map/ppermute | solution.py:107
  30.1 7.8 %collective-permute-start.6 = (bf16[144,512]{1,0:T(8,128)(2,1)S(1)}, bf16[144,512]{1,0:T(8,128)(2,1)S(1)}, u32[]{:S(2)}, u32[]{:S(2)}) collective-permute-start(bf16[144,512]{1,0:T(8,128)(2,1)S(1)} %get-tuple-element.22.s0), channel_id=1, source_target_pairs={{0,64},{4,68},{8,72},{12,76},{16,80},{20,84},{24,88},{28,92},{32,9... | collective-permute-start | bytes 442376 | tf_op jit(solution)/shard_map/ppermute | solution.py:103
  39.0 19.8 %collective-permute-start.9 = (bf16[528,512]{1,0:T(8,128)(2,1)S(1)}, bf16[528,512]{1,0:T(8,128)(2,1)S(1)}, u32[]{:S(2)}, u32[]{:S(2)}) collective-permute-start(bf16[528,512]{1,0:T(8,128)(2,1)S(1)} %get-tuple-element.27.a0), channel_id=1, source_target_pairs={{0,32},{4,36},{8,40},{12,44},{16,48},{20,52},{24,56},{28,60},{32,6... | collective-permute-start | bytes 1622024 | tf_op jit(solution)/shard_map/ppermute | solution.py:103
  40.6 18.9 %collective-permute-start.12 = (bf16[528,512]{1,0:T(8,128)(2,1)S(1)}, bf16[528,512]{1,0:T(8,128)(2,1)S(1)}, u32[]{:S(2)}, u32[]{:S(2)}) collective-permute-start(bf16[528,512]{1,0:T(8,128)(2,1)S(1)} %get-tuple-element.27.a0), channel_id=1, source_target_pairs={{0,96},{4,100},{8,104},{12,108},{16,112},{20,116},{24,120},{28,124... | collective-permute-start | bytes 1622024 | tf_op jit(solution)/shard_map/ppermute | solution.py:103
  41.1 17.7 %collective-permute-start.7 = (bf16[3,512,128]{2,1,0:T(8,128)(2,1)S(1)}, bf16[3,512,128]{2,1,0:T(8,128)(2,1)S(1)}, u32[]{:S(2)}, u32[]{:S(2)}) collective-permute-start(bf16[3,512,128]{2,1,0:T(8,128)(2,1)S(1)} %get-tuple-element.26.refs_0_), channel_id=1, source_target_pairs={{0,16},{4,20},{8,24},{12,28},{16,0},{20,4},{24,8},{28,12},{32,48},... | collective-permute-start | bytes 1179656 | tf_op jit(solution)/shard_map/ppermute | solution.py:103
  44.7 8.0 %collective-permute-start.10 = (bf16[144,512]{1,0:T(8,128)(2,1)S(1)}, bf16[144,512]{1,0:T(8,128)(2,1)S(1)}, u32[]{:S(2)}, u32[]{:S(2)}) collective-permute-start(bf16[144,512]{1,0:T(8,128)(2,1)S(1)} %collective-permute-done.6.needed.s0), channel_id=1, source_target_pairs={{0,2},{1,3},{2,0},{3,1},{4,6},{5,7},{6,4},{7,5},{8,10},{9,11},{10,... | collective-permute-start | bytes 442376 | tf_op jit(solution)/shard_map/ppermute | solution.py:107
  46.5 7.8 %collective-permute-start.13 = (bf16[144,512]{1,0:T(8,128)(2,1)S(1)}, bf16[144,512]{1,0:T(8,128)(2,1)S(1)}, u32[]{:S(2)}, u32[]{:S(2)}) collective-permute-start(bf16[144,512]{1,0:T(8,128)(2,1)S(1)} %collective-permute-done.6.needed.s0), channel_id=1, source_target_pairs={{0,1},{1,2},{2,3},{3,0},{4,5},{5,6},{6,7},{7,4},{8,9},{9,10},{10,1... | collective-permute-start | bytes 442376 | tf_op jit(solution)/shard_map/ppermute | solution.py:107
  52.8 5.1 %collective-permute-start.14 = (bf16[144,512]{1,0:T(8,128)(2,1)S(1)}, bf16[144,512]{1,0:T(8,128)(2,1)S(1)}, u32[]{:S(2)}, u32[]{:S(2)}) collective-permute-start(bf16[144,512]{1,0:T(8,128)(2,1)S(1)} %collective-permute-done.6.needed.s0), channel_id=1, source_target_pairs={{0,3},{1,0},{2,1},{3,2},{4,7},{5,4},{6,5},{7,6},{8,11},{9,8},{10,9... | collective-permute-start | bytes 442376 | tf_op jit(solution)/shard_map/ppermute | solution.py:107
  54.3 5.4 %collective-permute-start.8 = (bf16[528,512]{1,0:T(8,128)(2,1)S(1)}, bf16[528,512]{1,0:T(8,128)(2,1)S(1)}, u32[]{:S(2)}, u32[]{:S(2)}) collective-permute-start(bf16[528,512]{1,0:T(8,128)(2,1)S(1)} %get-tuple-element.27.a0), channel_id=1, source_target_pairs={{0,4},{4,0},{8,12},{12,8},{16,20},{20,16},{24,28},{28,24},{32,36},... | collective-permute-start | bytes 1622024 | tf_op jit(solution)/shard_map/ppermute | solution.py:103
  58.6 4.4 %collective-permute-start.16 = (bf16[528,512]{1,0:T(8,128)(2,1)S(1)}, bf16[528,512]{1,0:T(8,128)(2,1)S(1)}, u32[]{:S(2)}, u32[]{:S(2)}) collective-permute-start(bf16[528,512]{1,0:T(8,128)(2,1)S(1)} %shard_map.137.a2), channel_id=1, source_target_pairs={{0,4},{4,0},{8,12},{12,8},{16,20},{20,16},{24,28},{28,24},{32,36},... | collective-permute-start | bytes 1622024 | tf_op jit(solution)/shard_map/ppermute | solution.py:103
  58.9 4.0 %collective-permute-start.11 = (bf16[528,512]{1,0:T(8,128)(2,1)S(1)}, bf16[528,512]{1,0:T(8,128)(2,1)S(1)}, u32[]{:S(2)}, u32[]{:S(2)}) collective-permute-start(bf16[528,512]{1,0:T(8,128)(2,1)S(1)} %shard_map.135.a1), channel_id=1, source_target_pairs={{0,4},{4,0},{8,12},{12,8},{16,20},{20,16},{24,28},{28,24},{32,36},... | collective-permute-start | bytes 1622024 | tf_op jit(solution)/shard_map/ppermute | solution.py:103
  59.5 3.4 %collective-permute-start.15 = (bf16[528,512]{1,0:T(8,128)(2,1)S(1)}, bf16[528,512]{1,0:T(8,128)(2,1)S(1)}, u32[]{:S(2)}, u32[]{:S(2)}) collective-permute-start(bf16[528,512]{1,0:T(8,128)(2,1)S(1)} %shard_map.136.a3), channel_id=1, source_target_pairs={{0,4},{4,0},{8,12},{12,8},{16,20},{20,16},{24,28},{28,24},{32,36},... | collective-permute-start | bytes 1622024 | tf_op jit(solution)/shard_map/ppermute | solution.py:103
  59.7 17.4 %collective-permute-start.18 = (bf16[3,512,128]{2,1,0:T(8,128)(2,1)S(1)}, bf16[3,512,128]{2,1,0:T(8,128)(2,1)S(1)}, u32[]{:S(2)}, u32[]{:S(2)}) collective-permute-start(bf16[3,512,128]{2,1,0:T(8,128)(2,1)S(1)} %get-tuple-element.26.refs_0_), channel_id=1, source_target_pairs={{0,8},{4,12},{8,16},{12,20},{16,24},{20,28},{24,0},{28,4},{32,40},... | collective-permute-start | bytes 1179656 | tf_op jit(solution)/shard_map/ppermute | solution.py:103
  59.7 17.3 %collective-permute-start.19 = (bf16[3,512,128]{2,1,0:T(8,128)(2,1)S(1)}, bf16[3,512,128]{2,1,0:T(8,128)(2,1)S(1)}, u32[]{:S(2)}, u32[]{:S(2)}) collective-permute-start(bf16[3,512,128]{2,1,0:T(8,128)(2,1)S(1)} %get-tuple-element.26.refs_0_), channel_id=1, source_target_pairs={{0,24},{4,28},{8,0},{12,4},{16,8},{20,12},{24,16},{28,20},{32,56},... | collective-permute-start | bytes 1179656 | tf_op jit(solution)/shard_map/ppermute | solution.py:103
  76.7 17.2 %collective-permute-start.17 = (bf16[1664,128]{1,0:T(8,128)(2,1)S(1)}, bf16[1664,128]{1,0:T(8,128)(2,1)S(1)}, u32[]{:S(2)}, u32[]{:S(2)}) collective-permute-start(bf16[1664,128]{1,0:T(8,128)(2,1)S(1)} %get-tuple-element.33), channel_id=1, source_target_pairs={{0,16},{4,20},{8,24},{12,28},{16,0},{20,4},{24,8},{28,12},{32,48},... | collective-permute-start | bytes 1277960 | tf_op jit(solution)/shard_map/ppermute | solution.py:103
  91.8 11.7 %collective-permute-start.20 = (bf16[1664,128]{1,0:T(8,128)(2,1)S(1)}, bf16[1664,128]{1,0:T(8,128)(2,1)S(1)}, u32[]{:S(2)}, u32[]{:S(2)}) collective-permute-start(bf16[1664,128]{1,0:T(8,128)(2,1)S(1)} %get-tuple-element.34), channel_id=1, source_target_pairs={{0,24},{4,28},{8,0},{12,4},{16,8},{20,12},{24,16},{28,20},{32,56},... | collective-permute-start | bytes 1277960 | tf_op jit(solution)/shard_map/ppermute | solution.py:103
  93.3 12.5 %collective-permute-start.21 = (bf16[1664,128]{1,0:T(8,128)(2,1)S(1)}, bf16[1664,128]{1,0:T(8,128)(2,1)S(1)}, u32[]{:S(2)}, u32[]{:S(2)}) collective-permute-start(bf16[1664,128]{1,0:T(8,128)(2,1)S(1)} %get-tuple-element.35), channel_id=1, source_target_pairs={{0,8},{4,12},{8,16},{12,20},{16,24},{20,28},{24,0},{28,4},{32,40},... | collective-permute-start | bytes 1277960 | tf_op jit(solution)/shard_map/ppermute | solution.py:103

commit v3 on v2

--- a/solution.py
+++ b/solution.py
@@ -194,14 +194,14 @@
 
 
 def newest_kernel(
-    cur_ref, gain_hbm, weight_hbm, embed_hbm, qkv_hbm, part_ref, embed_out, qkv_out,
+    cur_ref, gain_hbm, weight_hbm, qkv_hbm, part_ref, qkv_out,
     act, gain_ref, weight_ref, sems,
 ):
     (gain_copy,) = fetch([gain_hbm], [gain_ref], sems)
     weight_copies = fetch(
         [weight_hbm.at[2, r] for r in range(3)], [weight_ref.at[r] for r in range(3)], sems, 1
     )
-    copies = fetch((embed_hbm, qkv_hbm), (embed_out, qkv_out), sems, 4)
+    copies = fetch([qkv_hbm], [qkv_out], sems, 4)
     place = lax.broadcasted_iota(jnp.int32, (80, 512), 0) % 8
     gain_copy.wait()
     for slot in range(2):
@@ -221,33 +221,32 @@
         copy.wait()
 
 
-def conv_newest(cur, norm_gain, conv_weight, embed_weight, qkv):
+def conv_newest(cur, norm_gain, conv_weight, qkv):
     return pl.pallas_call(
         newest_kernel,
-        in_specs=[VMEM] + [HBM] * 4,
-        out_specs=[VMEM] + [ANY] * 2,
+        in_specs=[VMEM] + [HBM] * 3,
+        out_specs=[VMEM, ANY],
         out_shape=[
             jax.ShapeDtypeStruct((SHARD, 512), F32),
-            jax.ShapeDtypeStruct(embed_weight.shape, BF16),
             jax.ShapeDtypeStruct(qkv.shape, BF16),
         ],
         scratch_shapes=[
             pltpu.VMEM((3, 2, 80, 512), F32),
             pltpu.VMEM((1, 512), F32),
             pltpu.VMEM((3, 3, 512, 512), BF16),
-            pltpu.SemaphoreType.DMA((6,)),
+            pltpu.SemaphoreType.DMA((5,)),
         ],
         compiler_params=params(16),
         cost_estimate=pl.CostEstimate(
             flops=2 * 128 * 4608 * 512, bytes_accessed=15000000, transcendentals=0
         ),
-    )(*in_vmem(cur), *pinned(norm_gain[None], conv_weight, embed_weight, qkv))
+    )(*in_vmem(cur), *pinned(norm_gain[None], conv_weight, qkv))
 
 
 def conv_kernel(
-    info_ref, cur_ref, prev_ref, part_ref, embed_ref, gain_hbm, bias_hbm, embed_bias_hbm, weight_hbm,
-    out_ref, send_ref,
-    act, gain_ref, bias_ref, embed_bias_ref, weight_ref, sems,
+    info_ref, cur_ref, prev_ref, part_ref, gain_hbm, bias_hbm, embed_bias_hbm, weight_hbm, embed_hbm,
+    out_ref, send_ref, embed_out,
+    embed_ref, act, gain_ref, bias_ref, embed_bias_ref, weight_ref, sems,
 ):
     copies = fetch(
         (gain_hbm, bias_hbm, embed_bias_hbm), (gain_ref, bias_ref, embed_bias_ref), sems
@@ -256,6 +255,7 @@
     weight_copies = fetch(
         [weight_hbm.at[tap] for tap in taps], [weight_ref.at[tap] for tap in taps], sems, 3
     )
+    (embed_copy,) = fetch([embed_hbm], [embed_ref], sems, 9)
     first_frame = info_ref[4] * 2
     slots = []
     for i in range(2):
@@ -287,6 +287,8 @@
                 piece, weight_ref[tap_time, tap_row, tap_col], preferred_element_type=F32
             )
     section = total.astype(BF16)
+    embed_copy.wait()
+    (embed_sent,) = fetch([embed_ref], [embed_out], sems, 10)
     out_ref[...] = section.reshape(out_ref.shape)
     send_ref[0:SHARD, :] = section
     embedded = jnp.dot(section, embed_ref[...], preferred_element_type=F32) + embed_bias_ref[...]
@@ -298,33 +300,36 @@
     tail = jnp.concatenate([high, low, jnp.zeros((16, 256), F32)], axis=1)
     place = lax.broadcasted_iota(jnp.int32, (16, 512), 0)
     send_ref[SHARD : SHARD + 16, :] = jnp.where(place == 0, tail, 0.0).astype(BF16)
-
-
-def conv(info, cur, prev, part, norm_gain, conv_bias, embed_near, embed_bias, conv_weight):
+    embed_sent.wait()
+
+
+def conv(info, cur, prev, part, norm_gain, conv_bias, embed_weight, embed_bias, conv_weight):
     return pl.pallas_call(
         conv_kernel,
-        in_specs=[SMEM] + [VMEM] * 4 + [HBM] * 4,
-        out_specs=[VMEM] * 2,
+        in_specs=[SMEM] + [VMEM] * 3 + [HBM] * 5,
+        out_specs=[VMEM] * 2 + [ANY],
         out_shape=[
             jax.ShapeDtypeStruct((2, 8, 8, 512), BF16),
             jax.ShapeDtypeStruct((SHARD + 16, 512), BF16),
+            jax.ShapeDtypeStruct(embed_weight.shape, BF16),
         ],
         scratch_shapes=[
+            pltpu.VMEM(embed_weight.shape, BF16),
             pltpu.VMEM((3, 4, 80, 512), F32),
             pltpu.VMEM((1, 512), F32),
             pltpu.VMEM((1, 512), F32),
             pltpu.VMEM((1, 3072), F32),
             pltpu.VMEM((2, 3, 3, 512, 512), BF16),
-            pltpu.SemaphoreType.DMA((9,)),
-        ],
-        compiler_params=params(24),
+            pltpu.SemaphoreType.DMA((11,)),
+        ],
+        compiler_params=params(28),
         cost_estimate=pl.CostEstimate(
             flops=2 * 128 * 13824 * 512, bytes_accessed=12000000, transcendentals=0
         ),
     )(
         info,
-        *in_vmem(cur, prev, part, embed_near),
-        *pinned(norm_gain[None], conv_bias[None], embed_bias[None], conv_weight),
+        *in_vmem(cur, prev, part),
+        *pinned(norm_gain[None], conv_bias[None], embed_bias[None], conv_weight, embed_weight),
     )
 
 
@@ -691,9 +696,9 @@
     cur = jnp.concatenate([above, section_in, below], axis=1)
     prev = halo(cur, 1, 0)
     qkv = jnp.transpose(qkv_weight, (1, 2, 0, 3)).reshape(9, 3072, HD)
-    part, embed_near, qkv_near = conv_newest(cur, norm_gain, conv_weight, embed_weight, qkv)
-    section_out, send = conv(
-        info, cur, prev, part, norm_gain, conv_bias, embed_near, embed_bias, conv_weight
+    part, qkv_near = conv_newest(cur, norm_gain, conv_weight, qkv)
+    section_out, send, embed_near = conv(
+        info, cur, prev, part, norm_gain, conv_bias, embed_weight, embed_bias, conv_weight
     )
     wq, wk, wv, rows, cols = fold(
         embed_near, embed_bias, mod_shift, mod_scale, k_gain, qkv_near

time: 110 us -> 108 us (0.982); the launches traced: 108 us -> 108 us
  transfers between devices with their start and end apart: 22 -> 22, of which waited for: 8 -> 7; matrix products, arithmetic and copies ran while one was open for 2% -> 2% of each run, Pallas kernels for 44% -> 43%
where the time goes in v3:
time: 108 us
  Pallas kernels  56.6 us (52%)
  starting transfers between devices  28 us (26%)
  waiting for transfers between devices  19.7 us (18%)
  local copies, waits for them, and re-layouts  1.67 us (2%)
  other arithmetic  1.39 us (1%)
    pallas_call x2, Pallas kernels, attend_next(): pl.pallas_call(functools.partial(next_kernel, groups), in_specs=[SMEM, VM...  22.4 us
    ppermute x13, starting transfers between devices, shift_tm(): return lax.ppermute(block, 'tm', route)  14.1 us
    pallas_call x1, Pallas kernels, attend_first(): pl.pallas_call(first_kernel, in_specs=[SMEM] + [ANY] * 13, out_specs=[VME...  13.7 us
    ppermute x6, waiting for transfers between devices, shift_band(): return lax.ppermute(block, 'band', [(i, (i + db) % NB) for i in range(NB)])  11 us
    ppermute x6, starting transfers between devices, shift_band(): return lax.ppermute(block, 'band', [(i, (i + db) % NB) for i in range(NB)])  7.21 us
    pallas_call x1, Pallas kernels, conv(): pl.pallas_call(conv_kernel, in_specs=[SMEM] + [VMEM] * 3 + [HBM] * 5, out...  7.17 us
    ppermute x3, starting transfers between devices, halo(): return lax.ppermute(block, ('tm', 'band'), route)  6.67 us
    pallas_call x1, Pallas kernels, fold(): pl.pallas_call(fold_kernel, in_specs=[VMEM] * 6, out_specs=[VMEM] * 5, ou...  5.02 us
  transfers between devices with their start and end apart: 22, of which 7 were waited for; matrix products, arithmetic and copies ran while one was open for 2% of the time, Pallas kernels for 43%

profile of v3, /device:TPU:2, one launch (start us, length us, event | category | flops | bytes accessed | tf_op | source)
XLA Modules:
  0.0 108.2 jit_solution(14531985284971154427)
XLA Ops:
  0.6 0.7 fusion
  1.4 3.5 %collective-permute-start = (bf16[2,1,8,512]{3,2,1,0:T(8,128)(2,1)S(1)}, bf16[2,1,8,512]{3,2,1,0:T(8,128)(2,1)S(1)}, u32[]{:S(2)}, u32[]{:S(2)}) collective-permute-start(bf16[2,1,8,512]{3,2,1,0:T(8,128)(2,1)S(1)} %get-tuple-element.37), channel_id=1, source_target_pairs={{0,1},{1,2},{2,3},{4,5},{5,6},{6,7},{8,9},{9,10},{10,11},{12,13},{... | collective-permute-start | bytes 49160 | tf_op jit(solution)/shard_map/ppermute | solution.py:117
  4.8 1.3 %collective-permute-start.1 = (bf16[2,1,8,512]{3,2,1,0:T(8,128)(2,1)S(1)}, bf16[2,1,8,512]{3,2,1,0:T(8,128)(2,1)S(1)}, u32[]{:S(2)}, u32[]{:S(2)}) collective-permute-start(bf16[2,1,8,512]{3,2,1,0:T(8,128)(2,1)S(1)} %get-tuple-element.36), channel_id=1, source_target_pairs={{1,0},{2,1},{3,2},{5,4},{6,5},{7,6},{9,8},{10,9},{11,10},{13,12},{... | collective-permute-start | bytes 49160 | tf_op jit(solution)/shard_map/ppermute | solution.py:117
  6.8 0.9 constant_dynamic-update-slice_fusion.1
  7.7 2.7 %collective-permute-done.1 = bf16[2,1,8,512]{3,2,1,0:T(8,128)(2,1)S(1)} collective-permute-done((bf16[2,1,8,512]{3,2,1,0:T(8,128)(2,1)S(1)}, bf16[2,1,8,512]{3,2,1,0:T(8,128)(2,1)S(1)}, u32[]{:S(2)}, u32[]{:S(2)}) %collective-permute-start.1) | collective-permute-done | bytes 16416 | tf_op jit(solution)/shard_map/ppermute | solution.py:117
  10.5 1.9 %collective-permute-start.2 = (bf16[2,10,8,512]{3,2,1,0:T(8,128)(2,1)S(1)}, bf16[2,10,8,512]{3,2,1,0:T(8,128)(2,1)S(1)}, u32[]{:S(2)}, u32[]{:S(2)}) collective-permute-start(bf16[2,10,8,512]{3,2,1,0:T(8,128)(2,1)S(1)} %constant_dynamic-update-slice_fusion.cur_ref), channel_id=1, source_target_pairs={{0,4},{1,5},{2,6},{3,7},{4,8},{5,9},{6,10},{7,11},{8,12},{9,13},{1... | collective-permute-start | bytes 491528 | tf_op jit(solution)/shard_map/ppermute | solution.py:117
  12.4 0.7 pad_add_fusion.info_ref.band_ref
  13.1 4.5 %shard_map.131 = (f32[128,512]{1,0:T(8,128)S(1)}, bf16[9,3072,128]{2,1,0:T(8,128)(2,1)S(1)}) custom-call(bf16[2,10,8,512]{3,2,1,0:T(8,128)(2,1)S(1)} %constant_dynamic-update-slice_fusion.cur_ref, f32[1,512]{1,0:T(1,128)} %bitcast.21, bf16[3,3,3,512,512]{4,3,2,1,0:T(8,128)(2,1)} %weight_hbm.3, bf16[9,3072,128]{2,1,0:T(8,128)(2,1)} %bitcast.19), custom_call_target="tpu_custom_call" | custom-call | flops 603979776 | bytes 15000000 | tf_op jit(solution)/shard_map/pallas_call | solution.py:225
  17.6 1.6 %collective-permute-done.2.prev_ref = bf16[2,10,8,512]{3,2,1,0:T(8,128)(2,1)S(1)} collective-permute-done((bf16[2,10,8,512]{3,2,1,0:T(8,128)(2,1)S(1)}, bf16[2,10,8,512]{3,2,1,0:T(8,128)(2,1)S(1)}, u32[]{:S(2)}, u32[]{:S(2)}) %collective-permute-start.2) | collective-permute-done | bytes 163872 | tf_op jit(solution)/shard_map/ppermute | solution.py:117
  19.2 7.2 %shard_map.132 = (bf16[2,8,8,512]{3,2,1,0:T(8,128)(2,1)}, bf16[144,512]{1,0:T(8,128)(2,1)S(1)}, bf16[512,3072]{1,0:T(8,128)(2,1)S(1)}) custom-call(s32[6]{0:T(128)S(1)} %pad_add_fusion.info_ref.band_ref, bf16[2,10,8,512]{3,2,1,0:T(8,128)(2,1)S(1)} %constant_dynamic-update-slice_fusion.cur_ref, bf16[2,10,8,512]{3,2,1,0:T(8,128)(2,1)S(1)} %collective-permute-done.2.prev_ref, ...), custom_call_target="tpu_custom_call" | custom-call | flops 1811939328 | bytes 12000000 | tf_op jit(solution)/shard_map/pallas_call | solution.py:307
  26.4 1.7 %collective-permute-start.3 = (bf16[144,512]{1,0:T(8,128)(2,1)S(1)}, bf16[144,512]{1,0:T(8,128)(2,1)S(1)}, u32[]{:S(2)}, u32[]{:S(2)}) collective-permute-start(bf16[144,512]{1,0:T(8,128)(2,1)S(1)} %get-tuple-element.21.s0), channel_id=1, source_target_pairs={{0,1},{1,2},{2,3},{3,0},{4,5},{5,6},{6,7},{7,4},{8,9},{9,10},{10,1... | collective-permute-start | bytes 442376 | tf_op jit(solution)/shard_map/ppermute | solution.py:107
  28.1 1.7 %collective-permute-start.4 = (bf16[144,512]{1,0:T(8,128)(2,1)S(1)}, bf16[144,512]{1,0:T(8,128)(2,1)S(1)}, u32[]{:S(2)}, u32[]{:S(2)}) collective-permute-start(bf16[144,512]{1,0:T(8,128)(2,1)S(1)} %get-tuple-element.21.s0), channel_id=1, source_target_pairs={{0,3},{1,0},{2,1},{3,2},{4,7},{5,4},{6,5},{7,6},{8,11},{9,8},{10,9... | collective-permute-start | bytes 442376 | tf_op jit(solution)/shard_map/ppermute | solution.py:107
  29.7 1.7 %collective-permute-start.5 = (bf16[144,512]{1,0:T(8,128)(2,1)S(1)}, bf16[144,512]{1,0:T(8,128)(2,1)S(1)}, u32[]{:S(2)}, u32[]{:S(2)}) collective-permute-start(bf16[144,512]{1,0:T(8,128)(2,1)S(1)} %get-tuple-element.21.s0), channel_id=1, source_target_pairs={{0,2},{1,3},{2,0},{3,1},{4,6},{5,7},{6,4},{7,5},{8,10},{9,11},{10,... | collective-permute-start | bytes 442376 | tf_op jit(solution)/shard_map/ppermute | solution.py:107
  31.4 2.1 %collective-permute-start.6 = (bf16[144,512]{1,0:T(8,128)(2,1)S(1)}, bf16[144,512]{1,0:T(8,128)(2,1)S(1)}, u32[]{:S(2)}, u32[]{:S(2)}) collective-permute-start(bf16[144,512]{1,0:T(8,128)(2,1)S(1)} %get-tuple-element.21.s0), channel_id=1, source_target_pairs={{0,64},{4,68},{8,72},{12,76},{16,80},{20,84},{24,88},{28,92},{32,9... | collective-permute-start | bytes 442376 | tf_op jit(solution)/shard_map/ppermute | solution.py:103
  33.5 5.0 %shard_map.133 = (bf16[512,384]{1,0:T(8,128)(2,1)S(1)}, bf16[384,512]{1,0:T(8,128)(2,1)S(1)}, bf16[512,384]{1,0:T(8,128)(2,1)S(1)}, f32[8,1152]{1,0:T(8,128)S(1)}, f32[3,384,128]{2,1,0:T(8,128)S(1)}) custom-call(bf16[512,3072]{1,0:T(8,128)(2,1)S(1)} %get-tuple-element.22.embed_ref, f32[1,3072]{1,0:T(1,128)S(1)} %bitcast.15, f32[1,3072]{1,0:T(1,128)S(1)} %bitcast.16, ...), custom_call_target="tpu_custom_call" | custom-call | flops 3737124864 | bytes 12000000 | tf_op jit(solution)/shard_map/pallas_call | solution.py:161
  38.6 1.2 %shard_map.134 = (bf16[3,512,128]{2,1,0:T(8,128)(2,1)S(1)}, bf16[528,512]{1,0:T(8,128)(2,1)S(1)}) custom-call(s32[6]{0:T(128)S(1)} %pad_add_fusion.info_ref.band_ref, bf16[144,512]{1,0:T(8,128)(2,1)S(1)} %get-tuple-element.21.s0, bf16[144,512]{1,0:T(8,128)(2,1)S(1)} %collective-permute-done.3.s1, bf16[144,512]{1,0:T(8,128)(2,1)S(1)} %collective-permute-done.4.s3, ...), custom_call_target="tpu_custom_call" | custom-call | flops 201326592 | bytes 2000000 | tf_op jit(solution)/shard_map/pallas_call | solution.py:388
  39.8 1.3 %collective-permute-start.9 = (bf16[528,512]{1,0:T(8,128)(2,1)S(1)}, bf16[528,512]{1,0:T(8,128)(2,1)S(1)}, u32[]{:S(2)}, u32[]{:S(2)}) collective-permute-start(bf16[528,512]{1,0:T(8,128)(2,1)S(1)} %get-tuple-element.27.a0), channel_id=1, source_target_pairs={{0,32},{4,36},{8,40},{12,44},{16,48},{20,52},{24,56},{28,60},{32,6... | collective-permute-start | bytes 1622024 | tf_op jit(solution)/shard_map/ppermute | solution.py:103
  41.0 0.8 collective-permute-start.12
  41.9 3.3 %collective-permute-start.7 = (bf16[3,512,128]{2,1,0:T(8,128)(2,1)S(1)}, bf16[3,512,128]{2,1,0:T(8,128)(2,1)S(1)}, u32[]{:S(2)}, u32[]{:S(2)}) collective-permute-start(bf16[3,512,128]{2,1,0:T(8,128)(2,1)S(1)} %get-tuple-element.26.refs_0_), channel_id=1, source_target_pairs={{0,16},{4,20},{8,24},{12,28},{16,0},{20,4},{24,8},{28,12},{32,48},... | collective-permute-start | bytes 1179656 | tf_op jit(solution)/shard_map/ppermute | solution.py:103
  45.2 1.8 %collective-permute-start.10 = (bf16[144,512]{1,0:T(8,128)(2,1)S(1)}, bf16[144,512]{1,0:T(8,128)(2,1)S(1)}, u32[]{:S(2)}, u32[]{:S(2)}) collective-permute-start(bf16[144,512]{1,0:T(8,128)(2,1)S(1)} %collective-permute-done.6.needed.s0), channel_id=1, source_target_pairs={{0,2},{1,3},{2,0},{3,1},{4,6},{5,7},{6,4},{7,5},{8,10},{9,11},{10,... | collective-permute-start | bytes 442376 | tf_op jit(solution)/shard_map/ppermute | solution.py:107
  47.4 5.8 %collective-permute-done.10.refs_1_.s2 = bf16[144,512]{1,0:T(8,128)(2,1)S(1)} collective-permute-done((bf16[144,512]{1,0:T(8,128)(2,1)S(1)}, bf16[144,512]{1,0:T(8,128)(2,1)S(1)}, u32[]{:S(2)}, u32[]{:S(2)}) %collective-permute-start.10) | collective-permute-done | bytes 147488 | tf_op jit(solution)/shard_map/ppermute | solution.py:107
  53.2 1.5 %collective-permute-done.13.refs_0_.s1 = bf16[144,512]{1,0:T(8,128)(2,1)S(1)} collective-permute-done((bf16[144,512]{1,0:T(8,128)(2,1)S(1)}, bf16[144,512]{1,0:T(8,128)(2,1)S(1)}, u32[]{:S(2)}, u32[]{:S(2)}) %collective-permute-start.13) | collective-permute-done | bytes 147488 | tf_op jit(solution)/shard_map/ppermute | solution.py:107
  54.8 3.6 %collective-permute-done.14.refs_1_.s3 = bf16[144,512]{1,0:T(8,128)(2,1)S(1)} collective-permute-done((bf16[144,512]{1,0:T(8,128)(2,1)S(1)}, bf16[144,512]{1,0:T(8,128)(2,1)S(1)}, u32[]{:S(2)}, u32[]{:S(2)}) %collective-permute-start.14) | collective-permute-done | bytes 147488 | tf_op jit(solution)/shard_map/ppermute | solution.py:107
  58.4 0.7 shard_map.137.a2
  60.2 3.2 %collective-permute-start.19 = (bf16[3,512,128]{2,1,0:T(8,128)(2,1)S(1)}, bf16[3,512,128]{2,1,0:T(8,128)(2,1)S(1)}, u32[]{:S(2)}, u32[]{:S(2)}) collective-permute-start(bf16[3,512,128]{2,1,0:T(8,128)(2,1)S(1)} %get-tuple-element.26.refs_0_), channel_id=1, source_target_pairs={{0,24},{4,28},{8,0},{12,4},{16,8},{20,12},{24,16},{28,20},{32,56},... | collective-permute-start | bytes 1179656 | tf_op jit(solution)/shard_map/ppermute | solution.py:103
  63.4 13.7 %shard_map.138 = (bf16[1664,128]{1,0:T(8,128)(2,1)S(1)}, bf16[3,128,4096]{2,1,0:T(8,128)(2,1)S(1)}, bf16[3,4096,128]{2,1,0:T(8,128)(2,1)S(1)}) custom-call(s32[6]{0:T(128)S(1)} %pad_add_fusion.info_ref.band_ref, bf16[3,512,128]{2,1,0:T(8,128)(2,1)S(1)} %collective-permute-done.7.refs_0_.q_hbm, bf16[528,512]{1,0:T(8,128)(2,1)S(1)} %get-tuple-element.27.a0, ...), custom_call_target="tpu_custom_call" | custom-call | flops 15000000512 | bytes 10000000 | tf_op jit(solution)/shard_map/pallas_call | solution.py:567
  77.5 14.7 %shard_map.140 = (bf16[1664,128]{1,0:T(8,128)(2,1)S(1)}, bf16[1664,128]{1,0:T(8,128)(2,1)S(1)}) custom-call(s32[6]{0:T(128)S(1)} %pad_add_fusion.info_ref.band_ref, bf16[3,128,4096]{2,1,0:T(8,128)(2,1)S(1)} %get-tuple-element.31.key_t, bf16[3,4096,128]{2,1,0:T(8,128)(2,1)S(1)} %get-tuple-element.32.value, ...), custom_call_target="tpu_custom_call" | custom-call | flops 16000000000 | bytes 8000000 | tf_op jit(solution)/shard_map/pallas_call | solution.py:623
  92.2 1.6 %collective-permute-start.20 = (bf16[1664,128]{1,0:T(8,128)(2,1)S(1)}, bf16[1664,128]{1,0:T(8,128)(2,1)S(1)}, u32[]{:S(2)}, u32[]{:S(2)}) collective-permute-start(bf16[1664,128]{1,0:T(8,128)(2,1)S(1)} %get-tuple-element.34), channel_id=1, source_target_pairs={{0,24},{4,28},{8,0},{12,4},{16,8},{20,12},{24,16},{28,20},{32,56},... | collective-permute-start | bytes 1277960 | tf_op jit(solution)/shard_map/ppermute | solution.py:103
  94.3 7.6 %shard_map.139.p0 = bf16[1664,128]{1,0:T(8,128)(2,1)S(1)} custom-call(s32[6]{0:T(128)S(1)} %pad_add_fusion.info_ref.band_ref, bf16[3,128,4096]{2,1,0:T(8,128)(2,1)S(1)} %get-tuple-element.31.key_t, bf16[3,4096,128]{2,1,0:T(8,128)(2,1)S(1)} %get-tuple-element.32.value, bf16[3,512,128]{2,1,0:T(8,128)(2,1)S(1)} %get-tuple-element.26.refs_0_, ...), custom_call_target="tpu_custom_call" | custom-call | flops 8000000000 | bytes 8000000 | tf_op jit(solution)/shard_map/pallas_call | solution.py:623
  101.9 1.9 %collective-permute-done.20.p1 = bf16[1664,128]{1,0:T(8,128)(2,1)S(1)} collective-permute-done((bf16[1664,128]{1,0:T(8,128)(2,1)S(1)}, bf16[1664,128]{1,0:T(8,128)(2,1)S(1)}, u32[]{:S(2)}, u32[]{:S(2)}) %collective-permute-start.20) | collective-permute-done | bytes 426016 | tf_op jit(solution)/shard_map/ppermute | solution.py:103
  103.9 2.4 %collective-permute-done.21.p2 = bf16[1664,128]{1,0:T(8,128)(2,1)S(1)} collective-permute-done((bf16[1664,128]{1,0:T(8,128)(2,1)S(1)}, bf16[1664,128]{1,0:T(8,128)(2,1)S(1)}, u32[]{:S(2)}, u32[]{:S(2)}) %collective-permute-start.21) | collective-permute-done | bytes 426016 | tf_op jit(solution)/shard_map/ppermute | solution.py:103
  106.2 1.9 %shard_map.141 = bf16[3,512,128]{2,1,0:T(8,128)(2,1)} custom-call(bf16[1664,128]{1,0:T(8,128)(2,1)S(1)} %shard_map.139.p0, bf16[1664,128]{1,0:T(8,128)(2,1)S(1)} %collective-permute-done.20.p1, bf16[1664,128]{1,0:T(8,128)(2,1)S(1)} %collective-permute-done.21.p2, bf16[1664,128]{1,0:T(8,128)(2,1)S(1)} %collective-permute-done.17.refs_1_.p3), custom_call_target="tpu_custom_call" | custom-call | tf_op jit(solution)/shard_map/pallas_call | solution.py:668
  (37 shorter events, 3.0 us)
Async XLA Ops:
  1.4 5.4 %collective-permute-start = (bf16[2,1,8,512]{3,2,1,0:T(8,128)(2,1)S(1)}, bf16[2,1,8,512]{3,2,1,0:T(8,128)(2,1)S(1)}, u32[]{:S(2)}, u32[]{:S(2)}) collective-permute-start(bf16[2,1,8,512]{3,2,1,0:T(8,128)(2,1)S(1)} %get-tuple-element.37), channel_id=1, source_target_pairs={{0,1},{1,2},{2,3},{4,5},{5,6},{6,7},{8,9},{9,10},{10,11},{12,13},{... | collective-permute-start | bytes 49160 | tf_op jit(solution)/shard_map/ppermute | solution.py:117
  4.8 5.6 %collective-permute-start.1 = (bf16[2,1,8,512]{3,2,1,0:T(8,128)(2,1)S(1)}, bf16[2,1,8,512]{3,2,1,0:T(8,128)(2,1)S(1)}, u32[]{:S(2)}, u32[]{:S(2)}) collective-permute-start(bf16[2,1,8,512]{3,2,1,0:T(8,128)(2,1)S(1)} %get-tuple-element.36), channel_id=1, source_target_pairs={{1,0},{2,1},{3,2},{5,4},{6,5},{7,6},{9,8},{10,9},{11,10},{13,12},{... | collective-permute-start | bytes 49160 | tf_op jit(solution)/shard_map/ppermute | solution.py:117
  10.5 8.7 %collective-permute-start.2 = (bf16[2,10,8,512]{3,2,1,0:T(8,128)(2,1)S(1)}, bf16[2,10,8,512]{3,2,1,0:T(8,128)(2,1)S(1)}, u32[]{:S(2)}, u32[]{:S(2)}) collective-permute-start(bf16[2,10,8,512]{3,2,1,0:T(8,128)(2,1)S(1)} %constant_dynamic-update-slice_fusion.cur_ref), channel_id=1, source_target_pairs={{0,4},{1,5},{2,6},{3,7},{4,8},{5,9},{6,10},{7,11},{8,12},{9,13},{1... | collective-permute-start | bytes 491528 | tf_op jit(solution)/shard_map/ppermute | solution.py:117
  19.2 14.3 %copy-start = (f32[3072]{0:T(1024)S(1)}, f32[3072]{0:T(1024)}, u32[]{:S(2)}) copy-start(f32[3072]{0:T(1024)} %param.18) | copy-start | bytes 36868
  19.2 14.3 %copy-start.1 = (f32[3072]{0:T(1024)S(1)}, f32[3072]{0:T(1024)}, u32[]{:S(2)}) copy-start(f32[3072]{0:T(1024)} %param.19) | copy-start | bytes 36868
  19.2 14.3 %copy-start.2 = (f32[3072]{0:T(1024)S(1)}, f32[3072]{0:T(1024)}, u32[]{:S(2)}) copy-start(f32[3072]{0:T(1024)} %param.20) | copy-start | bytes 36868
  19.2 14.3 %copy-start.3 = (f32[128]{0:T(128)S(1)}, f32[128]{0:T(128)}, u32[]{:S(2)}) copy-start(f32[128]{0:T(128)} %param.23) | copy-start | bytes 1540
  26.4 12.2 %collective-permute-start.3 = (bf16[144,512]{1,0:T(8,128)(2,1)S(1)}, bf16[144,512]{1,0:T(8,128)(2,1)S(1)}, u32[]{:S(2)}, u32[]{:S(2)}) collective-permute-start(bf16[144,512]{1,0:T(8,128)(2,1)S(1)} %get-tuple-element.21.s0), channel_id=1, source_target_pairs={{0,1},{1,2},{2,3},{3,0},{4,5},{5,6},{6,7},{7,4},{8,9},{9,10},{10,1... | collective-permute-start | bytes 442376 | tf_op jit(solution)/shard_map/ppermute | solution.py:107
  28.1 10.5 %collective-permute-start.4 = (bf16[144,512]{1,0:T(8,128)(2,1)S(1)}, bf16[144,512]{1,0:T(8,128)(2,1)S(1)}, u32[]{:S(2)}, u32[]{:S(2)}) collective-permute-start(bf16[144,512]{1,0:T(8,128)(2,1)S(1)} %get-tuple-element.21.s0), channel_id=1, source_target_pairs={{0,3},{1,0},{2,1},{3,2},{4,7},{5,4},{6,5},{7,6},{8,11},{9,8},{10,9... | collective-permute-start | bytes 442376 | tf_op jit(solution)/shard_map/ppermute | solution.py:107
  29.7 8.9 %collective-permute-start.5 = (bf16[144,512]{1,0:T(8,128)(2,1)S(1)}, bf16[144,512]{1,0:T(8,128)(2,1)S(1)}, u32[]{:S(2)}, u32[]{:S(2)}) collective-permute-start(bf16[144,512]{1,0:T(8,128)(2,1)S(1)} %get-tuple-element.21.s0), channel_id=1, source_target_pairs={{0,2},{1,3},{2,0},{3,1},{4,6},{5,7},{6,4},{7,5},{8,10},{9,11},{10,... | collective-permute-start | bytes 442376 | tf_op jit(solution)/shard_map/ppermute | solution.py:107
  31.4 7.2 %collective-permute-start.6 = (bf16[144,512]{1,0:T(8,128)(2,1)S(1)}, bf16[144,512]{1,0:T(8,128)(2,1)S(1)}, u32[]{:S(2)}, u32[]{:S(2)}) collective-permute-start(bf16[144,512]{1,0:T(8,128)(2,1)S(1)} %get-tuple-element.21.s0), channel_id=1, source_target_pairs={{0,64},{4,68},{8,72},{12,76},{16,80},{20,84},{24,88},{28,92},{32,9... | collective-permute-start | bytes 442376 | tf_op jit(solution)/shard_map/ppermute | solution.py:103
  39.8 19.5 %collective-permute-start.9 = (bf16[528,512]{1,0:T(8,128)(2,1)S(1)}, bf16[528,512]{1,0:T(8,128)(2,1)S(1)}, u32[]{:S(2)}, u32[]{:S(2)}) collective-permute-start(bf16[528,512]{1,0:T(8,128)(2,1)S(1)} %get-tuple-element.27.a0), channel_id=1, source_target_pairs={{0,32},{4,36},{8,40},{12,44},{16,48},{20,52},{24,56},{28,60},{32,6... | collective-permute-start | bytes 1622024 | tf_op jit(solution)/shard_map/ppermute | solution.py:103
  41.0 18.9 %collective-permute-start.12 = (bf16[528,512]{1,0:T(8,128)(2,1)S(1)}, bf16[528,512]{1,0:T(8,128)(2,1)S(1)}, u32[]{:S(2)}, u32[]{:S(2)}) collective-permute-start(bf16[528,512]{1,0:T(8,128)(2,1)S(1)} %get-tuple-element.27.a0), channel_id=1, source_target_pairs={{0,96},{4,100},{8,104},{12,108},{16,112},{20,116},{24,120},{28,124... | collective-permute-start | bytes 1622024 | tf_op jit(solution)/shard_map/ppermute | solution.py:103
  41.9 17.4 %collective-permute-start.7 = (bf16[3,512,128]{2,1,0:T(8,128)(2,1)S(1)}, bf16[3,512,128]{2,1,0:T(8,128)(2,1)S(1)}, u32[]{:S(2)}, u32[]{:S(2)}) collective-permute-start(bf16[3,512,128]{2,1,0:T(8,128)(2,1)S(1)} %get-tuple-element.26.refs_0_), channel_id=1, source_target_pairs={{0,16},{4,20},{8,24},{12,28},{16,0},{20,4},{24,8},{28,12},{32,48},... | collective-permute-start | bytes 1179656 | tf_op jit(solution)/shard_map/ppermute | solution.py:103
  45.2 8.1 %collective-permute-start.10 = (bf16[144,512]{1,0:T(8,128)(2,1)S(1)}, bf16[144,512]{1,0:T(8,128)(2,1)S(1)}, u32[]{:S(2)}, u32[]{:S(2)}) collective-permute-start(bf16[144,512]{1,0:T(8,128)(2,1)S(1)} %collective-permute-done.6.needed.s0), channel_id=1, source_target_pairs={{0,2},{1,3},{2,0},{3,1},{4,6},{5,7},{6,4},{7,5},{8,10},{9,11},{10,... | collective-permute-start | bytes 442376 | tf_op jit(solution)/shard_map/ppermute | solution.py:107
  47.0 7.8 %collective-permute-start.13 = (bf16[144,512]{1,0:T(8,128)(2,1)S(1)}, bf16[144,512]{1,0:T(8,128)(2,1)S(1)}, u32[]{:S(2)}, u32[]{:S(2)}) collective-permute-start(bf16[144,512]{1,0:T(8,128)(2,1)S(1)} %collective-permute-done.6.needed.s0), channel_id=1, source_target_pairs={{0,1},{1,2},{2,3},{3,0},{4,5},{5,6},{6,7},{7,4},{8,9},{9,10},{10,1... | collective-permute-start | bytes 442376 | tf_op jit(solution)/shard_map/ppermute | solution.py:107
  53.2 5.1 %collective-permute-start.14 = (bf16[144,512]{1,0:T(8,128)(2,1)S(1)}, bf16[144,512]{1,0:T(8,128)(2,1)S(1)}, u32[]{:S(2)}, u32[]{:S(2)}) collective-permute-start(bf16[144,512]{1,0:T(8,128)(2,1)S(1)} %collective-permute-done.6.needed.s0), channel_id=1, source_target_pairs={{0,3},{1,0},{2,1},{3,2},{4,7},{5,4},{6,5},{7,6},{8,11},{9,8},{10,9... | collective-permute-start | bytes 442376 | tf_op jit(solution)/shard_map/ppermute | solution.py:107
  54.8 5.4 %collective-permute-start.8 = (bf16[528,512]{1,0:T(8,128)(2,1)S(1)}, bf16[528,512]{1,0:T(8,128)(2,1)S(1)}, u32[]{:S(2)}, u32[]{:S(2)}) collective-permute-start(bf16[528,512]{1,0:T(8,128)(2,1)S(1)} %get-tuple-element.27.a0), channel_id=1, source_target_pairs={{0,4},{4,0},{8,12},{12,8},{16,20},{20,16},{24,28},{28,24},{32,36},... | collective-permute-start | bytes 1622024 | tf_op jit(solution)/shard_map/ppermute | solution.py:103
  59.0 4.4 %collective-permute-start.16 = (bf16[528,512]{1,0:T(8,128)(2,1)S(1)}, bf16[528,512]{1,0:T(8,128)(2,1)S(1)}, u32[]{:S(2)}, u32[]{:S(2)}) collective-permute-start(bf16[528,512]{1,0:T(8,128)(2,1)S(1)} %shard_map.137.a2), channel_id=1, source_target_pairs={{0,4},{4,0},{8,12},{12,8},{16,20},{20,16},{24,28},{28,24},{32,36},... | collective-permute-start | bytes 1622024 | tf_op jit(solution)/shard_map/ppermute | solution.py:103
  59.4 4.0 %collective-permute-start.11 = (bf16[528,512]{1,0:T(8,128)(2,1)S(1)}, bf16[528,512]{1,0:T(8,128)(2,1)S(1)}, u32[]{:S(2)}, u32[]{:S(2)}) collective-permute-start(bf16[528,512]{1,0:T(8,128)(2,1)S(1)} %shard_map.135.a1), channel_id=1, source_target_pairs={{0,4},{4,0},{8,12},{12,8},{16,20},{20,16},{24,28},{28,24},{32,36},... | collective-permute-start | bytes 1622024 | tf_op jit(solution)/shard_map/ppermute | solution.py:103
  60.0 3.4 %collective-permute-start.15 = (bf16[528,512]{1,0:T(8,128)(2,1)S(1)}, bf16[528,512]{1,0:T(8,128)(2,1)S(1)}, u32[]{:S(2)}, u32[]{:S(2)}) collective-permute-start(bf16[528,512]{1,0:T(8,128)(2,1)S(1)} %shard_map.136.a3), channel_id=1, source_target_pairs={{0,4},{4,0},{8,12},{12,8},{16,20},{20,16},{24,28},{28,24},{32,36},... | collective-permute-start | bytes 1622024 | tf_op jit(solution)/shard_map/ppermute | solution.py:103
  60.1 17.3 %collective-permute-start.18 = (bf16[3,512,128]{2,1,0:T(8,128)(2,1)S(1)}, bf16[3,512,128]{2,1,0:T(8,128)(2,1)S(1)}, u32[]{:S(2)}, u32[]{:S(2)}) collective-permute-start(bf16[3,512,128]{2,1,0:T(8,128)(2,1)S(1)} %get-tuple-element.26.refs_0_), channel_id=1, source_target_pairs={{0,8},{4,12},{8,16},{12,20},{16,24},{20,28},{24,0},{28,4},{32,40},... | collective-permute-start | bytes 1179656 | tf_op jit(solution)/shard_map/ppermute | solution.py:103
  60.2 17.3 %collective-permute-start.19 = (bf16[3,512,128]{2,1,0:T(8,128)(2,1)S(1)}, bf16[3,512,128]{2,1,0:T(8,128)(2,1)S(1)}, u32[]{:S(2)}, u32[]{:S(2)}) collective-permute-start(bf16[3,512,128]{2,1,0:T(8,128)(2,1)S(1)} %get-tuple-element.26.refs_0_), channel_id=1, source_target_pairs={{0,24},{4,28},{8,0},{12,4},{16,8},{20,12},{24,16},{28,20},{32,56},... | collective-permute-start | bytes 1179656 | tf_op jit(solution)/shard_map/ppermute | solution.py:103
  77.1 17.2 %collective-permute-start.17 = (bf16[1664,128]{1,0:T(8,128)(2,1)S(1)}, bf16[1664,128]{1,0:T(8,128)(2,1)S(1)}, u32[]{:S(2)}, u32[]{:S(2)}) collective-permute-start(bf16[1664,128]{1,0:T(8,128)(2,1)S(1)} %get-tuple-element.33), channel_id=1, source_target_pairs={{0,16},{4,20},{8,24},{12,28},{16,0},{20,4},{24,8},{28,12},{32,48},... | collective-permute-start | bytes 1277960 | tf_op jit(solution)/shard_map/ppermute | solution.py:103
  92.2 11.7 %collective-permute-start.20 = (bf16[1664,128]{1,0:T(8,128)(2,1)S(1)}, bf16[1664,128]{1,0:T(8,128)(2,1)S(1)}, u32[]{:S(2)}, u32[]{:S(2)}) collective-permute-start(bf16[1664,128]{1,0:T(8,128)(2,1)S(1)} %get-tuple-element.34), channel_id=1, source_target_pairs={{0,24},{4,28},{8,0},{12,4},{16,8},{20,12},{24,16},{28,20},{32,56},... | collective-permute-start | bytes 1277960 | tf_op jit(solution)/shard_map/ppermute | solution.py:103
  93.8 12.5 %collective-permute-start.21 = (bf16[1664,128]{1,0:T(8,128)(2,1)S(1)}, bf16[1664,128]{1,0:T(8,128)(2,1)S(1)}, u32[]{:S(2)}, u32[]{:S(2)}) collective-permute-start(bf16[1664,128]{1,0:T(8,128)(2,1)S(1)} %get-tuple-element.35), channel_id=1, source_target_pairs={{0,8},{4,12},{8,16},{12,20},{16,24},{20,28},{24,0},{28,4},{32,40},... | collective-permute-start | bytes 1277960 | tf_op jit(solution)/shard_map/ppermute | solution.py:103
